TPU v7x, 256 devices: a whole 4x4x8 slice. The times are simulated.
256 devices in a mesh: dp: 4 (over x_lo, core), fsdp: 64 (over z, y, x_hi).
Axes of the slice: x: 4 (x_hi: 2, x_lo: 2; x = x_hi * 2 + x_lo), y: 4, z: 8, core: 2. Of those that a mesh axis runs over, the one named last changes fastest.
Arguments:
- tokens: bfloat16 [98304, 5120], P(('dp', 'fsdp')), may hold values from -50 to 50
- codes: bfloat16 [5120, 1024], P('fsdp'), may hold values from -0.078125 to 0.078125
- scales: float32 [5120, 8], P('fsdp'), may hold values from 0.5 to 2
- norm_gain: float32 [1024], replicated, may hold values from 0.25 to 1.75
- key_grad: bfloat16 [98304, 1024], P(('dp', 'fsdp')), may hold values from -120 to 120
Outputs:
- keys: bfloat16 [98304, 1024], P(('dp', 'fsdp'))
- token_grad: bfloat16 [98304, 5120], P(('dp', 'fsdp'))
- weight_grad: float32 [5120, 1024], P('fsdp')
- gain_grad: float32 [1024], replicated
All inputs are finite; a program needn't handle non-finite values.
Results may differ from a plain program's by a relative error of at most 0.015.
Values may be sent and summed in bfloat16 or wider, within the bound.
A program may use at most 192 MiB of HBM per device.

v0:
```python
import jax
import jax.numpy as jnp
from jax import lax
from jax.sharding import PartitionSpec as P

BLOCK = 128


eps = 1e-06


def dequant(pieces):
    return (pieces[0].astype(jnp.float32) * jnp.repeat(pieces[1], BLOCK, axis=1)).astype(
        jnp.bfloat16
    )


def local(tokens, codes, scales, norm_gain, key_grad):
    gathered = (
        lax.all_gather(codes, "fsdp", axis=0, tiled=True),
        lax.all_gather(scales.astype(jnp.bfloat16), "fsdp", axis=0, tiled=True).astype(
            scales.dtype
        ),
    )
    weight = dequant(gathered)
    k_raw = jnp.dot(tokens, weight, preferred_element_type=jnp.float32)
    rinv = lax.rsqrt(jnp.mean(k_raw * k_raw, axis=1, keepdims=True) + eps)
    normed = k_raw * rinv
    keys = (normed * norm_gain).astype(jnp.bfloat16)
    grads = key_grad.astype(jnp.float32)
    gain_local = jnp.sum(grads * normed, axis=0)
    dnorm = grads * norm_gain
    d_raw = (rinv * (dnorm - normed * jnp.mean(dnorm * normed, axis=1, keepdims=True))).astype(
        jnp.bfloat16
    )
    token_grad = lax.dot_general(
        d_raw, weight, (((1,), (1,)), ((), ())), preferred_element_type=jnp.float32
    ).astype(jnp.bfloat16)
    partial_value = lax.dot_general(
        tokens, d_raw, (((0,), (0,)), ((), ())), preferred_element_type=jnp.float32
    ).astype(jnp.bfloat16)
    received = lax.all_to_all(partial_value[None], "fsdp", split_axis=1, concat_axis=0, tiled=True)
    group_sum = jnp.sum(received.astype(jnp.float32), axis=0)
    weight_grad = lax.psum(group_sum.astype(jnp.bfloat16), "dp").astype(jnp.float32)
    gain_grad = lax.psum(gain_local, ("dp", "fsdp"))
    return (keys, token_grad, weight_grad, gain_grad)


def solution(mesh):
    return jax.shard_map(
        local,
        mesh=mesh,
        in_specs=(
            P(("dp", "fsdp"), None),
            P("fsdp", None),
            P("fsdp", None),
            P(),
            P(("dp", "fsdp"), None),
        ),
        out_specs=(P(("dp", "fsdp"), None), P(("dp", "fsdp"), None), P("fsdp", None), P()),
        check_vma=False,
    )
```

profile of v0, /device:TPU:1, one launch (start us, length us, event | category | flops | bytes accessed | tf_op | source)
XLA Modules:
  0.0 751.7 jit_solution(7443126934408077)
XLA Ops:
  7.2 0.0 all-gather.3.cloned.1.call-start
  7.2 0.7 all-gather.3.cloned.1.call-update
  7.9 0.0 all-reduce.2.cloned.1.call-start
  7.9 1.5 copy.18
  9.4 0.7 convert_bitcast_fusion.1
  10.1 159.5 %all-gather = bf16[64,80,8]{1,2,0:T(8,128)(2,1)S(1)} all-gather(bf16[1,80,8]{1,2,0:T(8,128)(2,1)S(1)} %convert_bitcast_fusion.1), channel_id=1, replica_groups=mesh['dp'=4,'fsdp'=64] {'fsdp'}, dimensions={0}, use_global_device_ids=true | all-gather | bytes 83200 | tf_op jit(solution)/shard_map/all_gather | solution.py:21
  169.6 0.4 copy.21
  170.0 9.8 %all-gather.3.cloned.1.call-done = bf16[5120,1024]{1,0:T(8,128)(2,1)} async-done(((bf16[80,1024]{1,0:T(8,128)(2,1)}), bf16[5120,1024]{1,0:T(8,128)(2,1)}) %all-gather.3.cloned.1.call-update) | async-done | bytes 10485776 | tf_op jit(solution)/shard_map/all_gather | solution.py:20
  179.9 12.9 %broadcast_in_dim.4 = f32[5120,8,128]{2,1,0:T(8,128)} broadcast(f32[5120,8]{1,0:T(8,128)S(1)} %bitcast.37), dimensions={0,1} | broadcast | bytes 21135360 | tf_op jit(solution)/shard_map/broadcast_in_dim | solution.py:13
  192.8 0.0 copy-start.3
  192.8 17.7 %multiply_reduce_fusion = (f32[384]{0:T(512)S(1)}, f32[1024,384]{1,0:T(8,128)S(1)}) fusion(bf16[384,5120]{1,0:T(8,128)(2,1)} %param.5, f32[640,8,8,128]{3,2,1,0:T(8,128)} %bitcast.32, bf16[5120,1024]{1,0:T(8,128)(2,1)} %all-gather.3.cloned.1.call-done), kind=kOutput, calls=%fused_computation.15 | convolution fusion | flops 4043046400 | bytes 36963840 | tf_op jit(solution)/shard_map/dot_general | solution.py:26
  210.5 0.0 copy-start
  210.5 0.0 copy-done.3
  210.5 0.7 fusion.6
  211.2 0.5 fusion.5
  211.7 0.0 copy-start.1
  211.7 0.9 copy-done.1
  212.6 0.0 copy-done
  212.6 8.1 %convert_bitcast_fusion = bf16[1,5120,1024]{1,2,0:T(8,128)(2,1)} fusion(bf16[384,1024]{0,1:T(8,128)(2,1)S(1)} %get-tuple-element.18, bf16[384,5120]{1,0:T(8,128)(2,1)S(1)} %copy-done), kind=kOutput, calls=%fused_computation.2 | convolution fusion | flops 4031774720 | bytes 15204352 | tf_op jit(solution)/shard_map/dot_general | solution.py:39
  220.8 42.4 %copy.19 = bf16[1,5120,1024]{2,0,1:T(2,128)(2,1)} copy(bf16[1,5120,1024]{1,2,0:T(8,128)(2,1)} %convert_bitcast_fusion) | data formatting | bytes 20971520 | tf_op jit(solution)/shard_map/broadcast_in_dim | solution.py:42
  263.2 0.5 broadcast.25
  263.7 61.3 %reduce.4 = bf16[5120,1024]{1,0:T(8,128)(2,1)} reduce(bf16[5120,1,1024]{2,1,0:T(2,128)(2,1)} %bitcast.34, bf16[]{:T(256)} %broadcast.25), dimensions={1}, to_apply=%bitcast.24.reduce_sub_computation | reduce | bytes 20971522
  325.0 24.7 %reshape.31 = bf16[64,2,40960]{2,1,0:T(2,128)(2,1)} reshape(bf16[5120,1024]{1,0:T(8,128)(2,1)} %reduce.4) | data formatting | bytes 20971520
  349.7 221.2 %all_to_all.12 = bf16[64,2,40960]{2,1,0:T(2,128)(2,1)} all-to-all(bf16[64,2,40960]{2,1,0:T(2,128)(2,1)} %reshape.31), channel_id=1, replica_groups=mesh['dp'=4,'fsdp'=64] {'fsdp'}, dimensions={0} | all-to-all | bytes 20971520 | tf_op jit(solution)/shard_map/all_to_all | solution.py:42
  570.9 40.0 %reshape.32 = bf16[5120,1,1024]{2,1,0:T(2,128)(2,1)} reshape(bf16[64,2,40960]{2,1,0:T(2,128)(2,1)} %all_to_all.12) | data formatting | bytes 20971520
  610.9 15.1 %copy.23 = bf16[1,5120,1024]{2,1,0:T(8,128)(2,1)} copy(bf16[1,5120,1024]{2,0,1:T(2,128)(2,1)} %bitcast.35) | data formatting | bytes 20971520
  626.0 0.0 copy-start.2
  626.0 7.4 reduce_sum.41
  633.4 0.0 all-reduce.2.cloned.1.call-update
  633.4 0.0 copy-done.2
  633.4 16.3 %convolution_convert_fusion = bf16[384,5120]{1,0:T(8,128)(2,1)} fusion(bf16[384,1024]{0,1:T(8,128)(2,1)S(1)} %copy-done.2, f32[640,8,8,128]{3,2,1,0:T(8,128)} %bitcast.33, bf16[5120,1024]{1,0:T(8,128)(2,1)} %all-gather.3.cloned.1.call-done), kind=kOutput, calls=%fused_computation.3 | convolution fusion | flops 4044226560 | bytes 36175872 | tf_op jit(solution)/shard_map/dot_general | solution.py:36
  649.7 1.2 copy.20
  650.9 92.3 %psum.15 = f32[1024]{0:T(1024)} all-reduce(f32[1024]{0:T(1024)S(1)} %get-tuple-element.16), channel_id=1, replica_groups=mesh['dp'=4,'fsdp'=64] {'dp','fsdp'}, use_global_device_ids=true, to_apply=%region_5.0 | all-reduce | flops 1024 | bytes 8192 | tf_op jit(solution)/shard_map/psum | solution.py:45
  743.2 0.0 all-reduce.2.cloned.1.call-done
  743.2 1.7 convert_element_type.45
  (2 shorter events, 0.0 us)
Async XLA Ops:
  7.2 172.7 %all-gather.3.cloned.1.call-start = ((), (), s32[]{:S(2)}) async-start(), calls=%async_computation.1 | async-start | bytes 10649600 | tf_op jit(solution)/shard_map/all_gather | solution.py:20
  7.9 735.3 %all-reduce.2.cloned.1.call-start = ((), (), s32[]{:S(2)}) async-start(), calls=%async_computation.2 | async-start | bytes 327680 | tf_op jit(solution)/shard_map/psum | solution.py:44
  192.8 17.8 %copy-start.3 = (f32[1024]{0:T(1024)S(1)}, f32[1024]{0:T(1024)}, u32[]{:S(2)}) copy-start(f32[1024]{0:T(1024)} %param.8) | copy-start | bytes 12292
  210.5 2.1 copy-start
  211.7 0.9 copy-start.1
  626.0 7.4 copy-start.2
Sparse Core Ops, SparseCore 0:
  11.6 168.1 all-gather.2
  633.5 55.9 all-reduce.1
where the time goes:
time: 755 us; the launch traced here: 752 us
  blocking collectives  473 us (63%)
  local copies, waits for them, and re-layouts  140 us (19%)
  other arithmetic  72.2 us (10%)
  matrix products  42.2 us (6%)
  between operations  14.1 us (2%)
  waiting for transfers between devices  10.5 us (1%)
    all_to_all x1, blocking collectives, local(): lax.all_to_all(partial_value[None], 'fsdp', split_axis=1, concat_axis=0,...  221 us
    all_gather x1, blocking collectives, local(): lax.all_gather(scales.astype(jnp.bfloat16), 'fsdp', axis=0, tiled=True)  159 us
    psum x1, blocking collectives, local(): gain_grad = lax.psum(gain_local, ('dp', 'fsdp'))  92.3 us
    unnamed x14, local copies, waits for them, and re-layouts  83.9 us
    unnamed x2, other arithmetic  62 us
    broadcast_in_dim x1, local copies, waits for them, and re-layouts, local(): partial_value[None]  42.4 us
    dot_general x1, matrix products, local(): k_raw = jnp.dot(tokens, weight, preferred_element_type=jnp.float32)  17.7 us
    dot_general x1, matrix products, local(): lax.dot_general(d_raw, weight, (((1,), (1,)), ((), ())), preferred_elemen...  16.3 us
  transfers between devices with their start and end apart: 2, of which 1 were waited for; matrix products, arithmetic and copies ran while one was open for 3% of the time, Pallas kernels for 0%

commit v1 on v0

v1 whole, which is shorter than its diff:
```python
import jax
import jax.numpy as jnp
from jax import lax
from jax.experimental import pallas as pl
from jax.experimental.pallas import tpu as pltpu
from jax.sharding import PartitionSpec as P

MESH = pl.DeviceIdType.MESH
F32, BF16 = jnp.float32, jnp.bfloat16
BLOCK = 128
EPS = 1e-06
D, W, T, ROWS = 5120, 1024, 384, 80
HALF = W // 2
SLAB = 640
PAIR = 2 * SLAB
RA, RB, RC = 96, 96, 128
HA, HB, HC = RA // 2, RB // 2, RC // 2
OFF_A, OFF_B, OFF_C = 0, RA - ROWS, RA + RB - 2 * ROWS
NX, NY, NZ = 4, 4, 8


def segments(rows, block, offset, half):
    cuts = []
    for first, last, row, column in ((0, ROWS, 0, block), (ROWS, rows, offset, 3)):
        if first < half < last:
            cuts += [(first, half, row, column), (half, last, row + half - first, column)]
        else:
            cuts.append((first, last, row, column))
    return cuts


SEG_A = segments(RA, 0, OFF_A, HA)
SEG_B = segments(RB, 1, OFF_B, HB)
SEG_C = segments(RC, 2, OFF_C, HC)


def column(block):
    return pl.ds(block * BLOCK, BLOCK)


def rem(a, n):
    return lax.rem(a + 2 * n, n)


def add(*refs):
    total = refs[0][...].astype(F32)
    for ref in refs[1:]:
        total = total + ref[...].astype(F32)
    return total


def kernel(
    tokens, codes, scales, gain, key_grad,
    keys_out, tg_out, wg_out, gg_out,
    tokv, tokt, kgv, wf, wa, wb, wc, acc, draw, keyv, stats,
    ga, gb, gc, raf, ran, rb, rc, ray, rax, rbx, rbz, rcy, rcz, tgr, gsend, grecv, gfin, fin, stage,
    s_loc, s_out,
    s_d2d, r_d2d, s_ax, r_ax, s_ay, r_ay, s_az, r_az, s_z, r_z, s_bx, r_bx, s_cy, r_cy, s_ring, r_ring,
    s_raf, r_raf, s_ran, r_ran, s_rr, r_rr, s_one, r_one, s_gain, r_gain, s_fin, r_fin,
):
    dp, fs = lax.axis_index("dp"), lax.axis_index("fsdp")
    xl, core = dp // 2, lax.rem(dp, 2)
    z, y, xh = fs // 8, lax.rem(fs // 2, 4), lax.rem(fs, 2)
    x = xh * 2 + xl
    other = 1 - core
    sign = 2 * lax.rem(z, 2) - 1

    def dev(x_, y_, z_, c_):
        x_, y_, z_ = rem(x_, NX), rem(y_, NY), rem(z_, NZ)
        return (lax.rem(x_, 2) * 2 + c_, z_ * 8 + y_ * 2 + x_ // 2)

    def copy(src, dst, send, recv, device):
        return pltpu.make_async_remote_copy(
            src_ref=src, dst_ref=dst, send_sem=send, recv_sem=recv, device_id=device, device_id_type=MESH
        )

    def pair(k):
        return rem(z // 2 + sign * (k + k // 2 - 2 * (k // 3)), 4)

    def loop(n, body, first=0):
        lax.fori_loop(first, n, lambda i, c: (body(i), c)[1], 0)

    sib = dev(x, y, z, other)

    def c_tok(p):
        cols = pl.ds(p * PAIR, PAIR)
        return pltpu.make_async_copy(tokens.at[:, cols], tokv.at[pl.ds(core * T, T), cols], s_loc.at[p])

    def d_tok(p):
        cols = pl.ds(p * PAIR, PAIR)
        return copy(tokens.at[:, cols], tokv.at[pl.ds(core * T, T), cols], s_d2d.at[p], r_d2d.at[p], sib)

    def c_kg():
        return pltpu.make_async_copy(
            key_grad.at[:, pl.ds(core * HALF, HALF)], kgv.at[pl.ds(core * T, T)], s_loc.at[4]
        )

    def d_kg():
        return copy(
            key_grad.at[:, pl.ds(other * HALF, HALF)], kgv.at[pl.ds(core * T, T)], s_d2d.at[4], r_d2d.at[4], sib
        )

    def d_stats():
        return copy(stats.at[0], stats.at[1], s_d2d.at[5], r_d2d.at[5], sib)

    def d_keys():
        return copy(
            keyv.at[pl.ds(other * T, T)], keys_out.at[:, pl.ds(core * HALF, HALF)], s_d2d.at[6], r_d2d.at[6], sib
        )

    def c_keys():
        return pltpu.make_async_copy(
            keyv.at[pl.ds(core * T, T)], keys_out.at[:, pl.ds(core * HALF, HALF)], s_out.at[4]
        )

    def d_tg(p):
        cols = pl.ds(p * PAIR, PAIR)
        return copy(tokv.at[pl.ds(other * T, T), cols], tgr.at[:, cols], s_d2d.at[7 + p], r_d2d.at[7 + p], sib)

    def c_tg(p):
        cols = pl.ds(p * PAIR, PAIR)
        return pltpu.make_async_copy(tokv.at[pl.ds(core * T, T), cols], tg_out.at[:, cols], s_out.at[p])

    def m_ax():
        ref = wa.at[z, y, xh]
        return copy(ref, ref, s_ax.at[0], r_ax.at[0], dev(3 - x, y, z, core))

    def m_ay(j):
        ref = wa.at[z, y]
        return copy(ref, ref, s_ay.at[j - 1], r_ay.at[j - 1], dev(x, y + j, z, core))

    def m_az(d, s, h):
        sg = 1 - 2 * d
        ref = wa.at[rem(z - sg * s, NZ), pl.ds(2 * h, 2)]
        at = (s * 2 + h) * 2 + d
        return copy(ref, ref, s_az.at[at], r_az.at[at], dev(x, y, z + sg, core))

    def m_bz(j):
        ref = wb.at[y, z, xh, xl]
        return copy(ref, ref, s_z.at[j - 1], r_z.at[j - 1], dev(x, y, z + j, core))

    def m_cz(j):
        ref = wc.at[x, z, y]
        return copy(ref, ref, s_z.at[6 + j], r_z.at[6 + j], dev(x, y, z + j, core))

    def m_bx(k, j):
        ref = wb.at[y, pl.ds(2 * pair(k), 2), xh, xl]
        return copy(ref, ref, s_bx.at[k * 3 + j - 1], r_bx.at[k * 3 + j - 1], dev(x + j, y, z, core))

    def m_cy(k, j):
        ref = wc.at[x, pl.ds(2 * pair(k), 2), y]
        return copy(ref, ref, s_cy.at[k * 3 + j - 1], r_cy.at[k * 3 + j - 1], dev(x, y + j, z, core))

    def m_by(k, d, hop):
        sg = 1 - 2 * d
        if hop == 0:
            ref = wb.at[y, pl.ds(2 * pair(k), 2)]
        else:
            ref = wb.at[rem(y - sg, NY), 2 * pair(k) + d]
        at = (k * 2 + hop) * 2 + d
        return copy(ref, ref, s_ring.at[at], r_ring.at[at], dev(x, y + sg, z, core))

    def m_cx(k, d, hop):
        sg = 1 - 2 * d
        if hop == 0:
            ref = wc.at[x, pl.ds(2 * pair(k), 2)]
        else:
            ref = wc.at[rem(x - sg, NX), 2 * pair(k) + d]
        at = 16 + (k * 2 + hop) * 2 + d
        return copy(ref, ref, s_ring.at[at], r_ring.at[at], dev(x + sg, y, z, core))

    def m_f(d, s, first=False):
        sg = 1 - 2 * d
        src = ga.at[rem(z + 4, NZ), pl.ds(2 * d, 2)] if first else raf.at[d, s - 1]
        return copy(src, raf.at[d, s], s_raf.at[d * 4 + s], r_raf.at[d * 4 + s], dev(x, y, z + sg, core))

    def m_n(d, s, first=False):
        sg = 1 - 2 * d
        src = ga.at[rem(z + 3 * sg, NZ), pl.ds(2 * (1 - d), 2)] if first else ran.at[d, s - 2]
        return copy(src, ran.at[d, s - 1], s_ran.at[d * 3 + s - 1], r_ran.at[d * 3 + s - 1], dev(x, y, z + sg, core))

    def m_rb(k, d, what):
        sg = 1 - 2 * d
        q = pair(3 - k)
        src = (
            gb.at[rem(y + 2, NY), 2 * q + d],
            gb.at[rem(y + sg, NY), 2 * q + 1 - d],
            rb.at[k, d, 0],
        )[what]
        at = (k * 2 + d) * 3 + what
        return copy(src, rb.at[k, d, what], s_rr.at[at], r_rr.at[at], dev(x, y + sg, z, core))

    def m_rc(k, d, what):
        sg = 1 - 2 * d
        q = pair(3 - k)
        src = (
            gc.at[rem(x + 2, NX), 2 * q + d],
            gc.at[rem(x + sg, NX), 2 * q + 1 - d],
            rc.at[k, d, 0],
        )[what]
        at = 24 + (k * 2 + d) * 3 + what
        return copy(src, rc.at[k, d, what], s_rr.at[at], r_rr.at[at], dev(x + sg, y, z, core))

    def m_rbx(k, j):
        to = rem(x + j, NX)
        zs = pl.ds(2 * pair(3 - k), 2)
        at = k * 3 + j - 1
        return copy(
            gb.at[y, zs, to // 2, lax.rem(to, 2)], rbx.at[j - 1, zs], s_one.at[at], r_one.at[at], dev(to, y, z, core)
        )

    def m_rcy(k, j):
        to = rem(y + j, NY)
        zs = pl.ds(2 * pair(3 - k), 2)
        at = 12 + k * 3 + j - 1
        return copy(gc.at[x, zs, to], rcy.at[j - 1, zs], s_one.at[at], r_one.at[at], dev(x, to, z, core))

    def m_rbz(j):
        to = rem(z + j, NZ)
        at = 23 + j
        return copy(gb.at[y, to, xh, xl], rbz.at[j - 1], s_one.at[at], r_one.at[at], dev(x, y, to, core))

    def m_rcz(j):
        to = rem(z + j, NZ)
        at = 30 + j
        return copy(gc.at[x, to, y], rcz.at[j - 1], s_one.at[at], r_one.at[at], dev(x, y, to, core))

    def m_ray(j):
        to = rem(y + j, NY)
        at = 37 + j
        return copy(ga.at[z, to], ray.at[j - 1], s_one.at[at], r_one.at[at], dev(x, to, z, core))

    def m_rax(j):
        to = rem(x + j, NX)
        at = 40 + j
        src = ga.at[z, y, to // 2, pl.ds(lax.rem(to, 2) * HA, HA)]
        return copy(src, rax.at[j - 1], s_one.at[at], r_one.at[at], dev(to, y, z, core))

    def m_gx(j):
        return copy(gsend.at[0], grecv.at[j - 1], s_gain.at[j - 1], r_gain.at[j - 1], dev(x + j, y, z, core))

    def m_gy(j):
        return copy(gsend.at[1], grecv.at[2 + j], s_gain.at[2 + j], r_gain.at[2 + j], dev(x, y + j, z, core))

    def m_gz(j):
        return copy(gsend.at[2], grecv.at[5 + j], s_gain.at[5 + j], r_gain.at[5 + j], dev(x, y, z + j, core))

    def m_gs():
        return copy(gfin.at[core], gfin.at[core], s_gain.at[13], r_gain.at[13], sib)

    partner = x + 1 - 2 * xl
    fins = (dev(partner, y, z, core), sib, dev(partner, y, z, other))

    def m_fin(i):
        return copy(fin.at[xl, core], fin.at[xl, core], s_fin.at[i], r_fin.at[i], fins[i])

    loop(4, lambda p: c_tok(p).start())
    c_kg().start()

    barrier = pltpu.get_barrier_semaphore()

    def signal(device):
        pl.semaphore_signal(barrier, inc=1, device_id=device, device_id_type=MESH)

    loop(NX, lambda j: signal(dev(x + j, y, z, core)), 1)
    loop(NY, lambda j: signal(dev(x, y + j, z, core)), 1)
    loop(NZ, lambda j: signal(dev(x, y, z + j, core)), 1)
    signal(sib)
    signal(fins[2])

    for b in range(4):
        scale = jnp.where(core == 0, scales[:, b : b + 1], scales[:, 4 + b : 5 + b])
        code = codes[:, pl.ds(pl.multiple_of(core * HALF + b * BLOCK, BLOCK), BLOCK)]
        stage[:, column(b)] = (code.astype(F32) * scale).astype(BF16)
    for first, last, row, block in SEG_A:
        wa[z, y, xh, first:last] = stage[row : row + last - first, column(block)]
    for mine in range(2):

        @pl.when(xl == mine)
        def _():
            for first, last, row, block in SEG_B:
                if first // HB == mine:
                    wb[y, z, xh, mine, first - mine * HB : last - mine * HB] = stage[row : row + last - first, column(block)]
            for first, last, row, block in SEG_C:
                if first // HC == mine:
                    wc[x, z, y, first - mine * HC : last - mine * HC] = stage[row : row + last - first, column(block)]

    pl.semaphore_wait(barrier, 15)
    m_ax().start()
    loop(NZ, lambda j: m_cz(j).start(), 1)
    loop(NZ, lambda j: m_bz(j).start(), 1)
    d_kg().start()
    loop(4, lambda k: d_tok(pair(k)).start())

    m_ax().wait_recv()
    loop(NY, lambda j: m_ay(j).start(), 1)
    loop(NZ, lambda j: m_cz(j).wait_recv(), 1)
    loop(4, lambda k: loop(NY, lambda j: m_cy(k, j).start(), 1))
    loop(NY, lambda j: m_ay(j).wait_recv(), 1)
    for d in range(2):
        m_az(d, 0, d).start()
    for d in range(2):
        m_az(d, 0, 1 - d).start()
    loop(NZ, lambda j: m_bz(j).wait_recv(), 1)
    loop(4, lambda k: loop(NX, lambda j: m_bx(k, j).start(), 1))

    def own_rings(k):
        loop(NY, lambda j: m_cy(k, j).wait_recv(), 1)
        for d in range(2):
            m_cx(k, d, 0).start()
        loop(NX, lambda j: m_bx(k, j).wait_recv(), 1)
        for d in range(2):
            m_by(k, d, 0).start()

    loop(4, own_rings)
    acc[...] = jnp.zeros_like(acc)
    loop(4, lambda p: c_tok(p).wait())
    c_kg().wait()
    d_kg().wait_recv()

    def consume(k):
        for d in range(2):
            m_cx(k, d, 1).wait_recv()
            m_by(k, d, 1).wait_recv()
        p = pair(k)

        def rows_of(i):
            zz, yy, hh = 2 * p + i // 8, lax.rem(i // 2, 4), lax.rem(i, 2)
            base = zz * SLAB + yy * 160 + hh * ROWS
            for first, last, row, block in SEG_A:
                wf[pl.ds(pl.multiple_of(base + row, 16), last - first), column(block)] = wa[zz, yy, hh, first:last]
            for first, last, row, block in SEG_B:
                at = first // HB
                wf[pl.ds(pl.multiple_of(base + row, 16), last - first), column(block)] = wb[
                    yy, zz, hh, at, first - at * HB : last - at * HB
                ]
            for first, last, row, block in SEG_C:
                at = first // HC
                wf[pl.ds(pl.multiple_of(base + row, 16), last - first), column(block)] = wc[
                    2 * hh + at, zz, yy, first - at * HC : last - at * HC
                ]

        loop(16, rows_of)
        begin = pl.multiple_of(p * PAIR, BLOCK)
        acc[...] += jnp.dot(tokv[:, pl.ds(begin, PAIR)], wf[pl.ds(begin, PAIR), :], preferred_element_type=F32)

    def transpose(k):
        d_tok(pair(k)).wait_recv()

        def part(i):
            begin = pl.multiple_of(pair(k) * PAIR + i * 256, BLOCK)
            tokt[pl.ds(begin, 256), :] = tokv[:, pl.ds(begin, 256)].T

        loop(5, part)

    def ring(k):
        transpose(k)
        for d in range(2):
            m_cx(k, d, 0).wait_recv()
            m_cx(k, d, 1).start()
            m_by(k, d, 0).wait_recv()
            m_by(k, d, 1).start()
        for d in range(2):
            m_az(d, k, d).wait_recv()

            @pl.when(k < 3)
            def _():
                m_az(d, k + 1, d).start()

        @pl.when(k < 3)
        def _():
            for d in range(2):
                m_az(d, k, 1 - d).wait_recv()

                @pl.when(k < 2)
                def _():
                    m_az(d, k + 1, 1 - d).start()

        @pl.when(k > 0)
        def _():
            consume(k - 1)

    loop(4, ring)
    consume(3)

    gains = gain[0:1, pl.ds(pl.multiple_of(core * HALF, BLOCK), HALF)]
    lane = lax.broadcasted_iota(jnp.int32, (8, BLOCK), 1)
    CH = 64
    stats[0] = jnp.zeros((2, 8, BLOCK), F32)

    def sums(i):
        rows = pl.ds(pl.multiple_of(i * CH, CH), CH)
        k_raw = acc[rows, :]
        dn = kgv[rows, :].astype(F32) * gains
        one = jnp.sum(k_raw * k_raw, axis=1, keepdims=True)
        two = jnp.sum(dn * k_raw, axis=1, keepdims=True)
        for j in range(CH // 8):
            here = lane == i * (CH // 8) + j
            stats[0, 0] = jnp.where(here, one[8 * j : 8 * j + 8], stats[0, 0])
            stats[0, 1] = jnp.where(here, two[8 * j : 8 * j + 8], stats[0, 1])

    loop(2 * T // CH, sums)
    d_stats().start()
    d_stats().wait_recv()
    stats[2] = (stats[0] + stats[1]) * (1.0 / W)
    gsend[0] = jnp.zeros((8, HALF), F32)

    def factors(i):
        rinvs, means = [], []
        for j in range(CH // 8):
            here = lane == i * (CH // 8) + j
            rinv = lax.rsqrt(jnp.sum(jnp.where(here, stats[2, 0], 0.0), axis=1, keepdims=True) + EPS)
            rinvs.append(rinv)
            means.append(rinv * jnp.sum(jnp.where(here, stats[2, 1], 0.0), axis=1, keepdims=True))
        return jnp.concatenate(rinvs, axis=0), jnp.concatenate(means, axis=0)

    def norm(i):
        rows = pl.ds(pl.multiple_of(i * CH, CH), CH)
        rinv, mean = factors(i)
        normed = acc[rows, :] * rinv
        grads = kgv[rows, :].astype(F32)
        draw[rows, :] = (rinv * (grads * gains - normed * mean)).astype(BF16)
        keyv[rows, :] = (normed * gains).astype(BF16)
        gsend[0] += jnp.sum((grads * normed).reshape(CH // 8, 8, HALF), axis=0)

    loop(2 * T // CH, norm)

    def grad(k):
        q = pair(3 - k)

        def slab(i):
            zz = 2 * q + i
            begin = pl.multiple_of(zz * SLAB, BLOCK)
            part = jnp.dot(tokt[pl.ds(begin, SLAB), :], draw[...], preferred_element_type=F32).astype(BF16)
            for yy in range(NY):
                for hh in range(2):
                    base = yy * 160 + hh * ROWS
                    for first, last, row, block in SEG_A:
                        value = part[base + row : base + row + last - first, block * BLOCK : (block + 1) * BLOCK]
                        ga[zz, yy, hh, first:last] = value
                    for first, last, row, block in SEG_B:
                        value = part[base + row : base + row + last - first, block * BLOCK : (block + 1) * BLOCK]
                        at = first // HB
                        gb[yy, zz, hh, at, first - at * HB : last - at * HB] = value
                    for first, last, row, block in SEG_C:
                        value = part[base + row : base + row + last - first, block * BLOCK : (block + 1) * BLOCK]
                        at = first // HC
                        gc[2 * hh + at, zz, yy, first - at * HC : last - at * HC] = value

        loop(2, slab)
        for d in range(2):
            m_rc(k, d, 0).start()
            m_rb(k, d, 0).start()

        @pl.when(k == 0)
        def _():
            for d in range(2):
                m_f(d, 0, True).start()

        @pl.when(k == 1)
        def _():
            for d in range(2):
                m_n(d, 1, True).start()

        for d in range(2):
            m_rc(k, d, 1).start()
            m_rb(k, d, 1).start()

    loop(4, grad)
    d_keys().start()
    c_keys().start()
    loop(NX, lambda j: m_gx(j).start(), 1)

    def finish(k):
        q = pair(3 - k)
        for d in range(2):
            m_rc(k, d, 1).wait_recv()
            m_rc(k, d, 2).wait_recv()
        for h in range(2):
            ref = gc.at[x, 2 * q + h]
            ref[...] = add(ref, rc.at[k, h, 2], rc.at[k, 1 - h, 1]).astype(BF16)
        loop(NY, lambda j: m_rcy(k, j).start(), 1)
        for d in range(2):
            m_rb(k, d, 1).wait_recv()
            m_rb(k, d, 2).wait_recv()
        for h in range(2):
            ref = gb.at[y, 2 * q + h]
            ref[...] = add(ref, rb.at[k, h, 2], rb.at[k, 1 - h, 1]).astype(BF16)
        loop(NX, lambda j: m_rbx(k, j).start(), 1)

    def token_part(p):
        begin = pl.multiple_of(p * PAIR, BLOCK)
        weight = wf[pl.ds(begin, PAIR), :]
        for to in (other, core):
            rows = pl.ds(pl.multiple_of(to * T, T), T)
            tokv[rows, pl.ds(begin, PAIR)] = lax.dot_general(
                draw[rows, :], weight, (((1,), (1,)), ((), ())), preferred_element_type=F32
            ).astype(BF16)
        d_tg(p).start()

    def reduce(k):
        for d in range(2):
            sg = 1 - 2 * d
            q = pair(3 - k)
            m_rc(k, d, 0).wait_recv()
            ref = rc.at[k, d, 0]
            ref[...] = add(ref, gc.at[rem(x + sg, NX), 2 * q + d]).astype(BF16)
            m_rc(k, d, 2).start()
            m_rb(k, d, 0).wait_recv()
            ref = rb.at[k, d, 0]
            ref[...] = add(ref, gb.at[rem(y + sg, NY), 2 * q + d]).astype(BF16)
            m_rb(k, d, 2).start()

        @pl.when(k < 3)
        def _():
            for d in range(2):
                sg = 1 - 2 * d
                m_f(d, k, True).wait_recv()
                ref = raf.at[d, k]
                ref[...] = add(ref, ga.at[rem(z + sg * (3 - k), NZ), pl.ds(2 * d, 2)]).astype(BF16)
                m_f(d, k + 1).start()

            @pl.when(k > 0)
            def _():
                for d in range(2):
                    sg = 1 - 2 * d
                    m_n(d, k, True).wait_recv()
                    ref = ran.at[d, k - 1]
                    ref[...] = add(ref, ga.at[rem(z + sg * (3 - k), NZ), pl.ds(2 * (1 - d), 2)]).astype(BF16)
                    m_n(d, k + 1).start()

        token_part(k)

        @pl.when(k > 0)
        def _():
            finish(k - 1)

    loop(4, reduce)
    loop(NX, lambda j: m_gx(j).wait_recv(), 1)
    gsend[1] = add(gsend.at[0], *(grecv.at[i] for i in range(3)))
    loop(NY, lambda j: m_gy(j).start(), 1)
    for d in range(2):
        m_f(d, 3, True).wait_recv()
        m_n(d, 3, True).wait_recv()
    for h in range(2):
        ref = ga.at[z, pl.ds(2 * h, 2)]
        ref[...] = add(ref, raf.at[h, 3], ran.at[1 - h, 2]).astype(BF16)
    loop(NY, lambda j: m_ray(j).start(), 1)
    finish(3)

    loop(NY, lambda j: m_ray(j).wait_recv(), 1)
    ref = ga.at[z, y]
    ref[...] = add(ref, *(ray.at[i] for i in range(3))).astype(BF16)
    loop(NX, lambda j: m_rax(j).start(), 1)
    loop(NY, lambda j: m_gy(j).wait_recv(), 1)
    gsend[2] = add(gsend.at[1], *(grecv.at[3 + i] for i in range(3)))
    loop(NZ, lambda j: m_gz(j).start(), 1)

    loop(4, lambda k: loop(NY, lambda j: m_rcy(k, j).wait_recv(), 1))

    def sum_c(zz):
        ref = gc.at[x, zz, y]
        ref[...] = add(ref, *(rcy.at[i, zz] for i in range(3))).astype(BF16)

    loop(NZ, sum_c)
    loop(NZ, lambda j: m_rcz(j).start(), 1)
    loop(4, lambda k: loop(NX, lambda j: m_rbx(k, j).wait_recv(), 1))

    def sum_b(zz):
        ref = gb.at[y, zz, xh, xl]
        ref[...] = add(ref, *(rbx.at[i, zz] for i in range(3))).astype(BF16)

    loop(NZ, sum_b)
    loop(NZ, lambda j: m_rbz(j).start(), 1)

    def token_sum(p):
        d_tg(p).wait()
        begin = pl.multiple_of(p * PAIR, BLOCK)
        cols = pl.ds(begin, PAIR)
        rows = pl.ds(pl.multiple_of(core * T, T), T)
        tokv[rows, cols] = (tokv[rows, cols].astype(F32) + tgr[:, cols].astype(F32)).astype(BF16)
        c_tg(p).start()

    loop(4, token_sum)

    loop(NX, lambda j: m_rax(j).wait_recv(), 1)
    mine = fin.at[xl, core]
    mine[0:HA] = add(ga.at[z, y, xh, pl.ds(pl.multiple_of(xl * HA, 16), HA)], *(rax.at[i] for i in range(3)))
    loop(NZ, lambda j: m_rcz(j).wait_recv(), 1)
    mine[HA + HB :] = add(gc.at[x, z, y], *(rcz.at[i] for i in range(7)))
    loop(NZ, lambda j: m_rbz(j).wait_recv(), 1)
    mine[HA : HA + HB] = add(gb.at[y, z, xh, xl], *(rbz.at[i] for i in range(7)))
    for i in range(3):
        m_fin(i).start()
    loop(NZ, lambda j: m_gz(j).wait_recv(), 1)
    total = add(gsend.at[2], *(grecv.at[6 + i] for i in range(7)))
    gfin[core] = jnp.broadcast_to(jnp.sum(total, axis=0, keepdims=True), (8, HALF))
    m_gs().start()

    m_ax().wait_send()

    def drain_y(j):
        m_ay(j).wait_send()
        m_ray(j).wait_send()
        m_gy(j).wait_send()

    def drain_x(j):
        m_rax(j).wait_send()
        m_gx(j).wait_send()

    def drain_z(j):
        m_bz(j).wait_send()
        m_cz(j).wait_send()
        m_rbz(j).wait_send()
        m_rcz(j).wait_send()
        m_gz(j).wait_send()

    loop(NY, drain_y, 1)
    loop(NX, drain_x, 1)
    loop(NZ, drain_z, 1)

    def drain(k):
        def inner(j):
            m_bx(k, j).wait_send()
            m_cy(k, j).wait_send()
            m_rbx(k, j).wait_send()
            m_rcy(k, j).wait_send()

        loop(4, inner, 1)
        for d in range(2):
            for hop in range(2):
                m_by(k, d, hop).wait_send()
                m_cx(k, d, hop).wait_send()
            for what in range(3):
                m_rb(k, d, what).wait_send()
                m_rc(k, d, what).wait_send()
            m_az(d, k, d).wait_send()

            @pl.when(k < 3)
            def _():
                m_az(d, k, 1 - d).wait_send()

        d_tok(k).wait_send()

    loop(4, drain)
    for d in range(2):
        for s in range(4):
            m_f(d, s, True).wait_send()
        for s in range(1, 4):
            m_n(d, s, True).wait_send()
    d_kg().wait_send()
    d_stats().wait_send()
    d_keys().wait()
    c_keys().wait()
    loop(4, lambda p: c_tg(p).wait())

    for i in range(3):
        m_fin(i).wait()
    m_gs().wait()
    for c in range(2):
        for half in range(2):
            for segs, at, size in ((SEG_A, 0, HA), (SEG_B, HA, HB), (SEG_C, HA + HB, HC)):
                for first, last, row, block in segs:
                    if first // size == half:
                        wg_out[row : row + last - first, column(4 * c + block)] = fin[
                            half, c, at + first - half * size : at + last - half * size
                        ]
        gg_out[:, c * HALF : (c + 1) * HALF] = gfin[c, 0:1]


def scratch():
    vmem, dma = pltpu.VMEM, pltpu.SemaphoreType.DMA
    both = lambda n: [dma((n,)), dma((n,))]
    buffers = [
        vmem((2 * T, D), BF16),
        vmem((D, 2 * T), BF16),
        vmem((2 * T, HALF), BF16),
        vmem((D, HALF), BF16),
        vmem((NZ, NY, 2, RA, BLOCK), BF16),
        vmem((NY, NZ, 2, 2, HB, BLOCK), BF16),
        vmem((NX, NZ, NY, HC, BLOCK), BF16),
        vmem((2 * T, HALF), F32),
        vmem((2 * T, HALF), BF16),
        vmem((2 * T, HALF), BF16),
        vmem((3, 2, 8, BLOCK), F32),
        vmem((NZ, NY, 2, RA, BLOCK), BF16),
        vmem((NY, NZ, 2, 2, HB, BLOCK), BF16),
        vmem((NX, NZ, NY, HC, BLOCK), BF16),
        vmem((2, 4, 2, 2, RA, BLOCK), BF16),
        vmem((2, 3, 2, 2, RA, BLOCK), BF16),
        vmem((4, 2, 3, 2, 2, HB, BLOCK), BF16),
        vmem((4, 2, 3, NY, HC, BLOCK), BF16),
        vmem((3, 2, RA, BLOCK), BF16),
        vmem((3, HA, BLOCK), BF16),
        vmem((3, NZ, HB, BLOCK), BF16),
        vmem((7, HB, BLOCK), BF16),
        vmem((3, NZ, HC, BLOCK), BF16),
        vmem((7, HC, BLOCK), BF16),
        vmem((T, D), BF16),
        vmem((3, 8, HALF), F32),
        vmem((13, 8, HALF), F32),
        vmem((2, 8, HALF), F32),
        vmem((2, 2, HA + HB + HC, BLOCK), F32),
        vmem((ROWS, HALF), BF16),
    ]
    semaphores = [dma((5,)), dma((5,))]
    for n in (11, 1, 3, 16, 14, 12, 12, 32, 8, 6, 48, 44, 14, 3):
        semaphores += both(n)
    return buffers + semaphores


def local(tokens, codes, scales, norm_gain, key_grad):
    hbm, vmem = pl.BlockSpec(memory_space=pl.ANY), pl.BlockSpec(memory_space=pltpu.VMEM)
    keys, token_grad, weight_grad, gain_grad = pl.pallas_call(
        kernel,
        out_shape=(
            jax.ShapeDtypeStruct((T, W), BF16),
            jax.ShapeDtypeStruct((T, D), BF16),
            jax.ShapeDtypeStruct((ROWS, W), F32),
            jax.ShapeDtypeStruct((1, W), F32),
        ),
        in_specs=[hbm, vmem, vmem, vmem, hbm],
        out_specs=(hbm, hbm, vmem, vmem),
        scratch_shapes=scratch(),
        compiler_params=pltpu.CompilerParams(collective_id=0, has_side_effects=True, vmem_limit_bytes=61 << 20),
        cost_estimate=pl.CostEstimate(flops=6 * T * D * W, bytes_accessed=12 << 20, transcendentals=0),
    )(tokens, codes, scales, norm_gain.reshape(1, W), key_grad)
    return keys, token_grad, weight_grad, gain_grad.reshape(W)


def solution(mesh):
    return jax.shard_map(
        local,
        mesh=mesh,
        in_specs=(P(("dp", "fsdp"), None), P("fsdp", None), P("fsdp", None), P(), P(("dp", "fsdp"), None)),
        out_specs=(P(("dp", "fsdp"), None), P(("dp", "fsdp"), None), P("fsdp", None), P()),
        check_vma=False,
    )
```

time: 755 us -> 113 us (0.15)
  blocking collectives: 473 us -> 0 us
  local copies, waits for them, and re-layouts: 140 us -> 9.11 us
  Pallas kernels: 0 us -> 103 us
  other arithmetic: 72.2 us -> 0 us
  matrix products: 42.2 us -> 0 us
  between operations: 14.1 us -> 0.64 us
  waiting for transfers between devices: 10.5 us -> 0 us
    all_to_all x1 -> x0, blocking collectives: 221 us -> none  [local(): lax.all_to_all(partial_value[None], 'fsdp', split_axis=1, concat_axis=0,...]
    all_gather x1 -> x0, blocking collectives: 159 us -> none  [local(): lax.all_gather(scales.astype(jnp.bfloat16), 'fsdp', axis=0, tiled=True)]
    pallas_call x0 -> x1, Pallas kernels: none -> 103 us  [local(): pl.pallas_call(kernel, out_shape=(jax.ShapeDtypeStruct((T, W), BF16), jax...]
    psum x1 -> x0, blocking collectives: 92.3 us -> none  [local(): gain_grad = lax.psum(gain_local, ('dp', 'fsdp'))]
    unnamed x14 -> x9, local copies, waits for them, and re-layouts: 83.9 us -> 9.11 us
    unnamed x2 -> x0, other arithmetic: 62 us -> none
    broadcast_in_dim x2 -> x0, local copies, waits for them, and re-layouts: 55.3 us -> none  [the longest x1 42.4 us: local(): partial_value[None]]
    dot_general x3 -> x0, matrix products: 42.2 us -> none  [the longest x1 17.7 us: local(): k_raw = jnp.dot(tokens, weight, preferred_element_type=jnp.float32)]
  transfers between devices with their start and end apart: 2 -> 0, of which waited for: 1 -> 0; matrix products, arithmetic and copies ran while one was open for 3% -> 0% of each run, Pallas kernels for 0% -> 0%
where the time goes in v1:
time: 113 us
  Pallas kernels  103 us (91%)
  local copies, waits for them, and re-layouts  9.11 us (8%)
    pallas_call x1, Pallas kernels, local(): pl.pallas_call(kernel, out_shape=(jax.ShapeDtypeStruct((T, W), BF16), jax...  103 us
    unnamed x9, local copies, waits for them, and re-layouts  9.11 us

profile of v1, /device:TPU:1, one launch (start us, length us, event | category | flops | bytes accessed | tf_op | source)
XLA Modules:
  0.0 113.0 jit_solution(11031226077511102636)
XLA Ops:
  0.6 1.4 %copy.9.scales = f32[80,8]{1,0:T(8,128)} copy(f32[80,8]{0,1:T(8,128)} %param.7) | data formatting | bytes 5120 | tf_op args[2]
  2.0 103.2 %shard_map.84 = (bf16[384,1024]{1,0:T(8,128)(2,1)}, bf16[384,5120]{1,0:T(8,128)(2,1)}, f32[80,1024]{1,0:T(8,128)}, f32[1,1024]{1,0:T(1,128)}) custom-call(bf16[384,5120]{1,0:T(8,128)(2,1)} %tokens.1, bf16[80,1024]{1,0:T(8,128)(2,1)} %codes.1, f32[80,8]{1,0:T(8,128)} %copy.9.scales, f32[1,1024]{1,0:T(1,128)} %bitcast.3, bf16[384,1024]{1,0:T(8,128)(2,1)} %key_grad.1), custom_call_target="tpu_custom_call" | custom-call | flops 12079595520 | bytes 12582912 | tf_op jit(solution)/shard_map/pallas_call | solution.py:714
  105.3 2.1 %copy.14 = bf16[384,1024]{1,0:T(8,128)(2,1)} copy(bf16[384,1024]{1,0:T(8,128)(2,1)} %get-tuple-element.16) | data formatting | bytes 1572864
  107.3 0.0 copy-start
  107.3 0.0 copy-start.1
  107.3 4.3 %copy.15 = bf16[384,5120]{1,0:T(8,128)(2,1)} copy(bf16[384,5120]{1,0:T(8,128)(2,1)} %get-tuple-element.17) | data formatting | bytes 7864320
  111.7 0.0 copy-done
  111.7 0.7 copy.16
  112.4 0.0 copy-done.1
  112.4 0.6 copy.17
Async XLA Ops:
  107.3 4.3 %copy-start = (f32[80,1024]{1,0:T(8,128)S(1)}, f32[80,1024]{1,0:T(8,128)}, u32[]{:S(2)}) copy-start(f32[80,1024]{1,0:T(8,128)} %get-tuple-element.18) | copy-start | bytes 983044
  107.3 5.1 %copy-start.1 = (f32[1,1024]{1,0:T(1,128)S(1)}, f32[1,1024]{1,0:T(1,128)}, u32[]{:S(2)}) copy-start(f32[1,1024]{1,0:T(1,128)} %get-tuple-element.11) | copy-start | bytes 12292

commit v2 on v1

v2 whole, which is shorter than its diff:
```python
import jax
import jax.numpy as jnp
from jax import lax
from jax.experimental import pallas as pl
from jax.experimental.pallas import tpu as pltpu
from jax.sharding import PartitionSpec as P

MESH = pl.DeviceIdType.MESH
F32, BF16 = jnp.float32, jnp.bfloat16
BLOCK = 128
EPS = 1e-06
D, W, T, ROWS = 5120, 1024, 384, 80
HALF = W // 2
SLAB = 640
PAIR = 2 * SLAB
RA, RB, RC = 96, 96, 128
GA, GB, GC = 96, 96, 128
NX, NY, NZ = 4, 4, 8
UNITS = (1, 2, 3, 0)


def segments(rows, block, offset, half):
    cuts = []
    for first, last, row, column in ((0, ROWS, 0, block), (ROWS, rows, offset, 3)):
        if first < half < last:
            cuts += [(first, half, row, column), (half, last, row + half - first, column)]
        else:
            cuts.append((first, last, row, column))
    return cuts


def parts(a, b, c):
    return (
        (segments(a, 0, 0, a // 2), a // 2),
        (segments(b, 1, a - ROWS, b // 2), b // 2),
        (segments(c, 2, a + b - 2 * ROWS, c // 2), c // 2),
    )


(SEG_A, HA), (SEG_B, HB), (SEG_C, HC) = parts(RA, RB, RC)
(SEG_GA, HGA), (SEG_GB, HGB), (SEG_GC, HGC) = parts(GA, GB, GC)


def column(block):
    return pl.ds(block * BLOCK, BLOCK)


def rem(a, n):
    return lax.rem(a + 2 * n, n)


def add(*refs):
    total = refs[0][...].astype(F32)
    for ref in refs[1:]:
        total = total + ref[...].astype(F32)
    return total


def kernel(
    tokens, codes, scales, gain, key_grad,
    keys_out, tg_out, wg_out, gg_out,
    tokv, tokt, kgv, wf, wa, wb, wc, acc, draw, keyv, stats,
    ga, gb, gc, raa, rb, rc, ray, rax, rbx, rbz, rcy, rcz, tgr, gx, gy, gz, gfin, fin, stage,
    s_loc, s_out,
    s_d2d, r_d2d, s_ax, r_ax, s_ay, r_ay, s_az, r_az, s_z, r_z, s_bx, r_bx, s_cy, r_cy, s_by, r_by, s_cx, r_cx,
    s_raa, r_raa, s_rr, r_rr, s_one, r_one, s_gain, r_gain, s_fin, r_fin,
):
    dp, fs = lax.axis_index("dp"), lax.axis_index("fsdp")
    xl, core = dp // 2, lax.rem(dp, 2)
    z, y, xh = fs // 8, lax.rem(fs // 2, 4), lax.rem(fs, 2)
    x = xh * 2 + xl
    other = 1 - core
    sign = 2 * lax.rem(z, 2) - 1

    def dev(x_, y_, z_, c_):
        x_, y_, z_ = rem(x_, NX), rem(y_, NY), rem(z_, NZ)
        return (lax.rem(x_, 2) * 2 + c_, z_ * 8 + y_ * 2 + x_ // 2)

    def copy(src, dst, send, recv, device):
        return pltpu.make_async_remote_copy(
            src_ref=src, dst_ref=dst, send_sem=send, recv_sem=recv, device_id=device, device_id_type=MESH
        )

    def pair(k):
        return rem(z // 2 + sign * (k + k // 2 - 2 * (k // 3)), 4)

    def loop(n, body, first=0):
        lax.fori_loop(first, n, lambda i, c: (body(i), c)[1], 0)

    sib = dev(x, y, z, other)

    def c_tok(p):
        cols = pl.ds(p * PAIR, PAIR)
        return pltpu.make_async_copy(tokens.at[:, cols], tokv.at[pl.ds(core * T, T), cols], s_loc.at[p])

    def d_tok(p):
        cols = pl.ds(p * PAIR, PAIR)
        return copy(tokens.at[:, cols], tokv.at[pl.ds(core * T, T), cols], s_d2d.at[p], r_d2d.at[p], sib)

    def c_kg():
        return pltpu.make_async_copy(
            key_grad.at[:, pl.ds(core * HALF, HALF)], kgv.at[pl.ds(core * T, T)], s_loc.at[4]
        )

    def d_kg():
        return copy(
            key_grad.at[:, pl.ds(other * HALF, HALF)], kgv.at[pl.ds(core * T, T)], s_d2d.at[4], r_d2d.at[4], sib
        )

    def d_stats():
        return copy(stats.at[0], stats.at[1], s_d2d.at[5], r_d2d.at[5], sib)

    def d_keys():
        return copy(
            keyv.at[pl.ds(other * T, T)], keys_out.at[:, pl.ds(core * HALF, HALF)], s_d2d.at[6], r_d2d.at[6], sib
        )

    def c_keys():
        return pltpu.make_async_copy(
            keyv.at[pl.ds(core * T, T)], keys_out.at[:, pl.ds(core * HALF, HALF)], s_out.at[4]
        )

    def d_tg(p):
        cols = pl.ds(p * PAIR, PAIR)
        return copy(tokv.at[pl.ds(other * T, T), cols], tgr.at[:, cols], s_d2d.at[7 + p], r_d2d.at[7 + p], sib)

    def m_ax():
        return copy(wa.at[z, 0, 0], wa.at[z, 1, 0], s_ax.at[0], r_ax.at[0], dev(3 - x, y, z, core))

    def m_ay(u, j):
        at = u * 3 + j - 1
        return copy(wa.at[z, u, 0], wa.at[z, u, 4 - j], s_ay.at[at], r_ay.at[at], dev(x, y + j, z, core))

    def m_az(d, s, u):
        sg = 1 - 2 * d
        ref = wa.at[rem(z - sg * s, NZ), u]
        at = (s * 2 + u) * 2 + d
        return copy(ref, ref, s_az.at[at], r_az.at[at], dev(x, y, z + sg, core))

    def m_z(part, d, hops, begin):
        sg = 1 - 2 * d
        to = rem(z - sg * begin, NZ)
        ref = wc.at[x, to, 0] if part else wb.at[y, to, 0]
        at = ((part * 2 + d) * 2 + (begin > 0)) * 2 + (begin or hops) - 1
        return copy(ref, ref, s_z.at[at], r_z.at[at], dev(x, y, z + sg * hops, core))

    def m_bx(k, j):
        zs = pl.ds(2 * pair(k), 2)
        at = k * 3 + j - 1
        return copy(wb.at[y, zs, 0], wb.at[y, zs, 4 - j], s_bx.at[at], r_bx.at[at], dev(x + j, y, z, core))

    def m_cy(k, j):
        zs = pl.ds(2 * pair(k), 2)
        at = k * 3 + j - 1
        return copy(wc.at[x, zs, 0], wc.at[x, zs, 4 - j], s_cy.at[at], r_cy.at[at], dev(x, y + j, z, core))

    def long_ring(buf, me, k, unit, d, hop):
        slots = pl.ds(1, 3) if unit else pl.ds(0, 1)
        if hop == 0:
            return buf.at[me, pl.ds(2 * pair(k), 2), slots]
        return buf.at[rem(me - 1 + 2 * d, 4), 2 * pair(k) + d, slots]

    def m_by(k, unit, d, hop):
        ref = long_ring(wb, y, k, unit, d, hop)
        at = ((k * 2 + unit) * 2 + hop) * 2 + d
        return copy(ref, ref, s_by.at[at], r_by.at[at], dev(x, y + 1 - 2 * d, z, core))

    def m_cx(k, unit, d, hop):
        ref = long_ring(wc, x, k, unit, d, hop)
        at = ((k * 2 + unit) * 2 + hop) * 2 + d
        return copy(ref, ref, s_cx.at[at], r_cx.at[at], dev(x + 1 - 2 * d, y, z, core))

    def far(d, u):
        return u % 2 == 1 - d

    def m_a(d, u, s, first=False):
        sg = 1 - 2 * d
        src = ga.at[rem(z + sg * (4 - s), NZ), u] if first else raa.at[d, u, s - 1]
        at = (d * 4 + u) * 4 + s
        return copy(src, raa.at[d, u, s], s_raa.at[at], r_raa.at[at], dev(x, y, z + sg, core))

    def m_rb(k, d, what):
        sg = 1 - 2 * d
        q = pair(3 - k)
        src = (
            gb.at[rem(y + 2, NY), 2 * q + d],
            gb.at[rem(y + sg, NY), 2 * q + 1 - d],
            rb.at[k, d, 0],
        )[what]
        at = (k * 2 + d) * 3 + what
        return copy(src, rb.at[k, d, what], s_rr.at[at], r_rr.at[at], dev(x, y + sg, z, core))

    def m_rc(k, d, what):
        sg = 1 - 2 * d
        q = pair(3 - k)
        src = (
            gc.at[rem(x + 2, NX), 2 * q + d],
            gc.at[rem(x + sg, NX), 2 * q + 1 - d],
            rc.at[k, d, 0],
        )[what]
        at = 24 + (k * 2 + d) * 3 + what
        return copy(src, rc.at[k, d, what], s_rr.at[at], r_rr.at[at], dev(x + sg, y, z, core))

    def m_rbx(k, j):
        to = rem(x + j, NX)
        zs = pl.ds(2 * pair(3 - k), 2)
        at = k * 3 + j - 1
        return copy(
            gb.at[y, zs, to // 2, lax.rem(to, 2)], rbx.at[j - 1, zs], s_one.at[at], r_one.at[at], dev(to, y, z, core)
        )

    def m_rcy(k, j):
        to = rem(y + j, NY)
        zs = pl.ds(2 * pair(3 - k), 2)
        at = 12 + k * 3 + j - 1
        return copy(gc.at[x, zs, to], rcy.at[j - 1, zs], s_one.at[at], r_one.at[at], dev(x, to, z, core))

    def m_rz(part, d, s, first=False):
        sg = 1 - 2 * d
        to = rem(z + sg * (4 - s), NZ)
        own, held = (gc.at[x, to, y], rcz) if part else (gb.at[y, to, xh, xl], rbz)
        at = 24 + (part * 2 + d) * 4 + s
        return copy(own if first else held.at[d, s - 1], held.at[d, s], s_one.at[at], r_one.at[at], dev(x, y, z + sg, core))

    def m_ray(j):
        to = rem(y + j, NY)
        at = 39 + j
        return copy(ga.at[z, j], ray.at[j - 1], s_one.at[at], r_one.at[at], dev(x, to, z, core))

    def m_rax(j):
        to = rem(x + j, NX)
        at = 42 + j
        src = ga.at[z, 0, to // 2, pl.ds(lax.rem(to, 2) * HGA, HGA)]
        return copy(src, rax.at[j - 1], s_one.at[at], r_one.at[at], dev(to, y, z, core))

    def m_gx(j):
        ref = gx.at[x]
        return copy(ref, ref, s_gain.at[j - 1], r_gain.at[j - 1], dev(x + j, y, z, core))

    def m_gy(j):
        ref = gy.at[y]
        return copy(ref, ref, s_gain.at[2 + j], r_gain.at[2 + j], dev(x, y + j, z, core))

    def m_gz(d, s):
        sg = 1 - 2 * d
        ref = gz.at[rem(z - sg * s, NZ)]
        at = 6 + d * 4 + s
        return copy(ref, ref, s_gain.at[at], r_gain.at[at], dev(x, y, z + sg, core))

    def m_gs():
        return copy(gfin.at[core], gfin.at[core], s_gain.at[14], r_gain.at[14], sib)

    partner = x + 1 - 2 * xl
    fins = (dev(partner, y, z, core), sib, dev(partner, y, z, other))

    def m_fin(i):
        return copy(fin.at[xl, core], fin.at[xl, core], s_fin.at[i], r_fin.at[i], fins[i])

    loop(4, lambda p: c_tok(p).start())
    c_kg().start()

    barrier = pltpu.get_barrier_semaphore()

    def signal(device):
        pl.semaphore_signal(barrier, inc=1, device_id=device, device_id_type=MESH)

    loop(NX, lambda j: signal(dev(x + j, y, z, core)), 1)
    loop(NY, lambda j: signal(dev(x, y + j, z, core)), 1)
    for hops in (1, 2):
        signal(dev(x, y, z + hops, core))
        signal(dev(x, y, z - hops, core))
    signal(sib)
    signal(fins[2])

    scale_t = scales[...].T
    for b in range(4):
        scale = jnp.where(core == 0, scale_t[:, b : b + 1], scale_t[:, 4 + b : 5 + b])
        code = codes[:, pl.ds(pl.multiple_of(core * HALF + b * BLOCK, BLOCK), BLOCK)]
        stage[:, column(b)] = (code.astype(F32) * scale).astype(BF16)
    for first, last, row, block in SEG_A:
        wa[z, 0, 0, first:last] = stage[row : row + last - first, column(block)]
    for mine in range(2):

        @pl.when(xl == mine)
        def _():
            for first, last, row, block in SEG_B:
                if first // HB == mine:
                    wb[y, z, 0, first - mine * HB : last - mine * HB] = stage[row : row + last - first, column(block)]
            for first, last, row, block in SEG_C:
                if first // HC == mine:
                    wc[x, z, 0, first - mine * HC : last - mine * HC] = stage[row : row + last - first, column(block)]

    pl.semaphore_wait(barrier, 12)
    m_ax().start()
    for j in range(1, NY):
        m_ay(0, j).start()
    for part in (1, 0):
        for hops in (2, 1):
            for d in range(2):
                m_z(part, d, hops, 0).start()
    d_kg().start()
    loop(4, lambda k: d_tok(pair(k)).start())
    acc[...] = jnp.zeros_like(acc)
    loop(4, lambda p: c_tok(p).wait())
    c_kg().wait()
    d_kg().wait_recv()

    def consume(k):
        p = pair(k)

        def rows_of(i):
            zz, yy, hh = 2 * p + i // 8, lax.rem(i // 2, 4), lax.rem(i, 2)
            base = zz * SLAB + yy * 160 + hh * ROWS
            for first, last, row, block in SEG_A:
                wf[pl.ds(pl.multiple_of(base + row, 16), last - first), column(block)] = wa[
                    zz, (hh + xh) % 2, rem(yy - y, NY), first:last
                ]
            for first, last, row, block in SEG_B:
                at = first // HB
                wf[pl.ds(pl.multiple_of(base + row, 16), last - first), column(block)] = wb[
                    yy, zz, rem(2 * hh + at - x, NX), first - at * HB : last - at * HB
                ]
            for first, last, row, block in SEG_C:
                at = first // HC
                wf[pl.ds(pl.multiple_of(base + row, 16), last - first), column(block)] = wc[
                    2 * hh + at, zz, rem(yy - y, NY), first - at * HC : last - at * HC
                ]

        loop(16, rows_of)
        begin = pl.multiple_of(p * PAIR, BLOCK)
        acc[...] += jnp.dot(tokv[:, pl.ds(begin, PAIR)], wf[pl.ds(begin, PAIR), :], preferred_element_type=F32)

    def transpose(k):
        d_tok(pair(k)).wait_recv()

        def part(i):
            begin = pl.multiple_of(pair(k) * PAIR + i * 256, BLOCK)
            tokt[pl.ds(begin, 256), :] = tokv[:, pl.ds(begin, 256)].T

        loop(5, part)

    def own_columns(part, ks):
        for k in ks:
            for d in range(2):
                (m_cx if part else m_by)(k, 0, d, 0).start()
            for j in range(1, 4):
                (m_cy if part else m_bx)(k, j).start()

    def far_z(part, wait):
        for d, begin in ((0, 1), (1, 1), (1 - part, 2)):
            move = m_z(part, d, 2, begin)
            move.wait_recv() if wait else move.start()

    def columns(k):
        for j in range(1, NY):
            m_cy(k, j).wait_recv()
        for d in range(2):
            m_cx(k, 1, d, 0).start()
        for j in range(1, NX):
            m_bx(k, j).wait_recv()
        for d in range(2):
            m_by(k, 1, d, 0).start()

    def own_forward(k):
        for d in range(2):
            m_cx(k, 0, d, 0).wait_recv()
            m_cx(k, 0, d, 1).start()
            m_by(k, 0, d, 0).wait_recv()
            m_by(k, 0, d, 1).start()

    m_ax().wait_recv()
    for j in range(1, NY):
        m_ay(1, j).start()
    for part in (1, 0):
        for hops in (1, 2):
            for d in range(2):
                m_z(part, d, hops, 0).wait_recv()
        far_z(part, False)
        own_columns(part, (0, 1))
    for j in range(1, NY):
        m_ay(0, j).wait_recv()
    for d in range(2):
        m_az(d, 0, 0).start()
    far_z(1, True)
    own_columns(1, (2, 3))
    far_z(0, True)
    own_columns(0, (2, 3))
    for j in range(1, NY):
        m_ay(1, j).wait_recv()
    for d in range(2):
        m_az(d, 0, 1).start()
    for d in range(2):
        m_az(d, 0, 0).wait_recv()
        m_az(d, 1, 0).start()
    loop(2, columns)
    loop(2, own_forward)
    for d in range(2):
        m_az(d, 0, 1).wait_recv()
        m_az(d, 1, 1).start()

    def forward(k):
        for d in range(2):
            m_cx(k, 1, d, 0).wait_recv()
            m_cx(k, 1, d, 1).start()
            m_by(k, 1, d, 0).wait_recv()
            m_by(k, 1, d, 1).start()

    def later(k):
        columns(k)
        forward(k - 2)
        own_forward(k)

    loop(4, later, 2)

    def ring(k):
        for u in range(2):
            for d in range(2):

                @pl.when(k < 2 + (u == d))
                def _():
                    m_az(d, k + 1, u).wait_recv()

                @pl.when(k < 1 + (u == d))
                def _():
                    m_az(d, k + 2, u).start()

        @pl.when(k < 2)
        def _():
            forward(k + 2)

        transpose(k)

        @pl.when(k > 0)
        def _():
            last_hops(k - 1)
            consume(k - 1)

    def last_hops(k):
        for unit in range(2):
            for d in range(2):
                m_cx(k, unit, d, 1).wait_recv()
                m_by(k, unit, d, 1).wait_recv()

    loop(4, ring)
    last_hops(3)
    consume(3)

    gains = gain[0:1, pl.ds(pl.multiple_of(core * HALF, BLOCK), HALF)]
    lane = lax.broadcasted_iota(jnp.int32, (8, BLOCK), 1)
    CH = 64

    def sums(i, packed):
        rows = pl.ds(pl.multiple_of(i * CH, CH), CH)
        k_raw = acc[rows, :]
        dn = kgv[rows, :].astype(F32) * gains
        one = jnp.sum(k_raw * k_raw, axis=1, keepdims=True)
        two = jnp.sum(dn * k_raw, axis=1, keepdims=True)
        for j in range(CH // 8):
            here = lane == i * (CH // 8) + j
            packed = (
                jnp.where(here, one[8 * j : 8 * j + 8], packed[0]),
                jnp.where(here, two[8 * j : 8 * j + 8], packed[1]),
            )
        return packed

    nothing = jnp.zeros((8, BLOCK), F32)
    stats[0, 0], stats[0, 1] = lax.fori_loop(0, 2 * T // CH, sums, (nothing, nothing))
    d_stats().start()
    d_stats().wait_recv()
    stats[2] = (stats[0] + stats[1]) * (1.0 / W)
    gx[x] = jnp.zeros((8, HALF), F32)

    def factors(i):
        rinvs, means = [], []
        for j in range(CH // 8):
            here = lane == i * (CH // 8) + j
            rinv = lax.rsqrt(jnp.sum(jnp.where(here, stats[2, 0], 0.0), axis=1, keepdims=True) + EPS)
            rinvs.append(rinv)
            means.append(rinv * jnp.sum(jnp.where(here, stats[2, 1], 0.0), axis=1, keepdims=True))
        return jnp.concatenate(rinvs, axis=0), jnp.concatenate(means, axis=0)

    def norm(i):
        rows = pl.ds(pl.multiple_of(i * CH, CH), CH)
        rinv, mean = factors(i)
        draw[rows, :] = (rinv * (kgv[rows, :].astype(F32) * gains - acc[rows, :] * (rinv * mean))).astype(BF16)

    loop(2 * T // CH, norm)

    def norm_keys(i):
        rows = pl.ds(pl.multiple_of(i * CH, CH), CH)
        normed = acc[rows, :] * factors(i)[0]
        keyv[rows, :] = (normed * gains).astype(BF16)
        gx[x] += jnp.sum((kgv[rows, :].astype(F32) * normed).reshape(CH // 8, 8, HALF), axis=0)

    def grad(t):
        k = t // 2
        e = rem(z + t, 2)
        zz = 2 * pair(3 - k) + e
        begin = pl.multiple_of(zz * SLAB, BLOCK)
        part = jnp.dot(tokt[pl.ds(begin, SLAB), :], draw[...], preferred_element_type=F32).astype(BF16)
        for yy in range(NY):
            for hh in range(2):
                base = yy * 160 + hh * ROWS
                for first, last, row, block in SEG_GA:
                    value = part[base + row : base + row + last - first, block * BLOCK : (block + 1) * BLOCK]
                    ga[zz, rem(yy - y, NY), hh, first:last] = value
                for first, last, row, block in SEG_GB:
                    value = part[base + row : base + row + last - first, block * BLOCK : (block + 1) * BLOCK]
                    at = first // HGB
                    gb[yy, zz, hh, at, first - at * HGB : last - at * HGB] = value
                for first, last, row, block in SEG_GC:
                    value = part[base + row : base + row + last - first, block * BLOCK : (block + 1) * BLOCK]
                    at = first // HGC
                    gc[2 * hh + at, zz, yy, first - at * HGC : last - at * HGC] = value

        @pl.when(k < 2)
        def _():
            m_rc(k, e, 0).start()
            m_rb(k, e, 0).start()
            m_rc(k, 1 - e, 1).start()
            m_rb(k, 1 - e, 1).start()

        @pl.when(t == 0)
        def _():
            for u in UNITS:
                m_a(u % 2 ^ 1, u, 0, True).start()

        for at, d in ((1, 1 - lax.rem(z, 2)), (3, lax.rem(z, 2))):

            @pl.when(t == at)
            def _():
                for i in range(2):
                    m_a(d, d + 2 * i, 1, True).start()

    loop(8, grad)
    loop(2 * T // CH, norm_keys)
    d_keys().start()
    c_keys().start()
    loop(NX, lambda j: m_gx(j).start(), 1)

    def finish(k):
        q = pair(3 - k)
        for d in range(2):
            m_rc(k, d, 1).wait_recv()
            m_rc(k, d, 2).wait_recv()
        for h in range(2):
            ref = gc.at[x, 2 * q + h]
            ref[...] += rc[k, h, 2] + rc[k, 1 - h, 1]
        loop(NY, lambda j: m_rcy(k, j).start(), 1)
        for d in range(2):
            m_rb(k, d, 1).wait_recv()
            m_rb(k, d, 2).wait_recv()
        for h in range(2):
            ref = gb.at[y, 2 * q + h]
            ref[...] += rb[k, h, 2] + rb[k, 1 - h, 1]
        loop(NX, lambda j: m_rbx(k, j).start(), 1)

    def short(k):
        for j in range(1, NY):
            m_rcy(k, j).wait_recv()
            m_rbx(k, j).wait_recv()

        def slab(i):
            zz = 2 * pair(3 - k) + i
            ref = gc.at[x, zz, y]
            ref[...] = add(ref, *(rcy.at[i, zz] for i in range(3))).astype(BF16)
            ref = gb.at[y, zz, xh, xl]
            ref[...] = add(ref, *(rbx.at[i, zz] for i in range(3))).astype(BF16)

        loop(2, slab)
        for part, d in ((1, 0), (1, 1), (0, 0), (0, 1)):
            begin = 0 if part != d else 1
            to = rem(z + (1 - 2 * d) * (4 - k), NZ)

            @pl.when(k == begin)
            def _():
                m_rz(part, d, begin, True).start()

            @pl.when(k > begin)
            def _():
                m_rz(part, d, k - 1, True).wait_recv()
                if part:
                    rcz[d, k - 1] += gc[x, to, y]
                else:
                    rbz[d, k - 1] += gb[y, to, xh, xl]
                m_rz(part, d, k).start()

    def token_part(p):
        begin = pl.multiple_of(p * PAIR, BLOCK)
        weight = wf[pl.ds(begin, PAIR), :]
        for to in (other, core):
            rows = pl.ds(pl.multiple_of(to * T, T), T)
            tokv[rows, pl.ds(begin, PAIR)] = lax.dot_general(
                draw[rows, :], weight, (((1,), (1,)), ((), ())), preferred_element_type=F32
            ).astype(BF16)
        d_tg(p).start()

    def gain_step(s):
        for d in range(2):
            m_gz(d, s).wait_recv()
            m_gz(d, s + 1).start()

    def reduce(k):
        for d in range(2):
            sg = 1 - 2 * d
            q = pair(3 - k)
            m_rc(k, d, 0).wait_recv()
            ref = rc.at[k, d, 0]
            ref[...] += gc[rem(x + sg, NX), 2 * q + d]
            m_rc(k, d, 2).start()
            m_rb(k, d, 0).wait_recv()
            ref = rb.at[k, d, 0]
            ref[...] += gb[rem(y + sg, NY), 2 * q + d]
            m_rb(k, d, 2).start()

        @pl.when(k < 2)
        def _():
            for what in range(2):
                for d in range(2):
                    m_rc(k + 2, d, what).start()
                    m_rb(k + 2, d, what).start()

        for u in UNITS:
            for d in range(2):
                sg = 1 - 2 * d

                @pl.when((k < 3) & (k >= (0 if far(d, u) else 1)))
                def _():
                    m_a(d, u, k, True).wait_recv()
                    raa[d, u, k] += ga[rem(z + sg * (3 - k), NZ), u]
                    m_a(d, u, k + 1).start()

        token_part(k)

        @pl.when(k > 0)
        def _():
            finish(k - 1)

        @pl.when(k > 1)
        def _():
            short(k - 2)

        @pl.when(k == 0)
        def _():
            loop(NX, lambda j: m_gx(j).wait_recv(), 1)
            gy[y] = add(*(gx.at[i] for i in range(NX)))
            loop(NY, lambda j: m_gy(j).start(), 1)

        @pl.when(k == 1)
        def _():
            loop(NY, lambda j: m_gy(j).wait_recv(), 1)
            gz[z] = add(*(gy.at[i] for i in range(NY)))
            for d in range(2):
                m_gz(d, 0).start()

        @pl.when(k > 1)
        def _():
            gain_step(k - 2)

    loop(4, reduce)
    m_gz(0, 2).wait_recv()
    m_gz(1, 2).wait_recv()
    m_gz(0, 3).start()
    finish(3)
    short(2)
    for u in UNITS:
        for d in range(2):
            m_a(d, u, 3, True).wait_recv()
        ref = ga.at[z, u]
        ref[...] += raa[0, u, 3] + raa[1, u, 3]
        if u > 0:
            m_ray(u).start()

    loop(NY, lambda j: m_ray(j).wait_recv(), 1)
    ref = ga.at[z, 0]
    ref[...] = add(ref, *(ray.at[i] for i in range(3))).astype(BF16)
    loop(NX, lambda j: m_rax(j).start(), 1)
    short(3)

    m_gz(0, 3).wait_recv()
    total = add(*(gz.at[i] for i in range(NZ)))
    gfin[core] = jnp.broadcast_to(jnp.sum(total, axis=0, keepdims=True), (8, HALF))
    m_gs().start()

    def token_sum(p):
        d_tg(p).wait()
        begin = pl.multiple_of(p * PAIR, BLOCK)
        cols = pl.ds(begin, PAIR)
        rows = pl.ds(pl.multiple_of(core * T, T), T)
        tg_out[:, cols] = (tokv[rows, cols].astype(F32) + tgr[:, cols].astype(F32)).astype(BF16)

    loop(4, token_sum)

    loop(NX, lambda j: m_rax(j).wait_recv(), 1)
    mine = fin.at[xl, core]
    own = ga.at[z, 0, xh, pl.ds(pl.multiple_of(xl * HGA, 16), HGA)]
    mine[0:HGA] = add(own, *(rax.at[i] for i in range(3))).astype(BF16)
    for d in range(2):
        m_rz(1, d, 3).wait_recv()
    mine[HGA + HGB :] = add(gc.at[x, z, y], rcz.at[0, 3], rcz.at[1, 3]).astype(BF16)
    for d in range(2):
        m_rz(0, d, 3).wait_recv()
    mine[HGA : HGA + HGB] = add(gb.at[y, z, xh, xl], rbz.at[0, 3], rbz.at[1, 3]).astype(BF16)
    for i in range(3):
        m_fin(i).start()
    m_ax().wait_send()

    def drain_y(j):
        m_ray(j).wait_send()
        m_gy(j).wait_send()

    def drain_x(j):
        m_rax(j).wait_send()
        m_gx(j).wait_send()

    loop(NY, drain_y, 1)
    loop(NX, drain_x, 1)

    def drain(k):
        def inner(j):
            m_bx(k, j).wait_send()
            m_cy(k, j).wait_send()
            m_rbx(k, j).wait_send()
            m_rcy(k, j).wait_send()

        loop(4, inner, 1)
        for d in range(2):
            for hop in range(2):
                for unit in range(2):
                    m_by(k, unit, d, hop).wait_send()
                    m_cx(k, unit, d, hop).wait_send()
            for what in range(3):
                m_rb(k, d, what).wait_send()
                m_rc(k, d, what).wait_send()
            for u in range(2):

                @pl.when(k < 3 + (u == d))
                def _():
                    m_az(d, k, u).wait_send()

            for u in range(4):

                @pl.when(k >= (0 if far(d, u) else 1))
                def _():
                    m_a(d, u, k, True).wait_send()

            @pl.when(k < 4 - d)
            def _():
                m_gz(d, k).wait_send()

            @pl.when(k >= d)
            def _():
                m_rz(1, d, k, True).wait_send()

            @pl.when(k >= 1 - d)
            def _():
                m_rz(0, d, k, True).wait_send()

        d_tok(k).wait_send()

    loop(4, drain)
    for u in range(2):
        for j in range(1, NY):
            m_ay(u, j).wait_send()
    for part in range(2):
        for d, hops, begin in ((0, 1, 0), (1, 1, 0), (0, 2, 0), (1, 2, 0), (0, 2, 1), (1, 2, 1), (1 - part, 2, 2)):
            m_z(part, d, hops, begin).wait_send()
    d_kg().wait_send()
    d_stats().wait_send()
    d_keys().wait()
    c_keys().wait()

    for i in range(3):
        m_fin(i).wait()
    m_gs().wait()
    for c in range(2):
        for half in range(2):
            for segs, at, size in ((SEG_GA, 0, HGA), (SEG_GB, HGA, HGB), (SEG_GC, HGA + HGB, HGC)):
                for first, last, row, block in segs:
                    if first // size == half:
                        wg_out[row : row + last - first, column(4 * c + block)] = fin[
                            half, c, at + first - half * size : at + last - half * size
                        ].astype(F32)
        gg_out[:, c * HALF : (c + 1) * HALF] = gfin[c, 0:1]


def scratch():
    vmem, dma = pltpu.VMEM, pltpu.SemaphoreType.DMA
    both = lambda n: [dma((n,)), dma((n,))]
    buffers = [
        vmem((2 * T, D), BF16),
        vmem((D, 2 * T), BF16),
        vmem((2 * T, HALF), BF16),
        vmem((D, HALF), BF16),
        vmem((NZ, 2, NY, RA, BLOCK), BF16),
        vmem((NY, NZ, NX, HB, BLOCK), BF16),
        vmem((NX, NZ, NY, HC, BLOCK), BF16),
        vmem((2 * T, HALF), F32),
        vmem((2 * T, HALF), BF16),
        vmem((2 * T, HALF), BF16),
        vmem((3, 2, 8, BLOCK), F32),
        vmem((NZ, NY, 2, GA, BLOCK), BF16),
        vmem((NY, NZ, 2, 2, HGB, BLOCK), BF16),
        vmem((NX, NZ, NY, HGC, BLOCK), BF16),
        vmem((2, 4, 4, 2, GA, BLOCK), BF16),
        vmem((4, 2, 3, 2, 2, HGB, BLOCK), BF16),
        vmem((4, 2, 3, NY, HGC, BLOCK), BF16),
        vmem((3, 2, GA, BLOCK), BF16),
        vmem((3, HGA, BLOCK), BF16),
        vmem((3, NZ, HGB, BLOCK), BF16),
        vmem((2, 4, HGB, BLOCK), BF16),
        vmem((3, NZ, HGC, BLOCK), BF16),
        vmem((2, 4, HGC, BLOCK), BF16),
        vmem((T, D), BF16),
        vmem((NX, 8, HALF), F32),
        vmem((NY, 8, HALF), F32),
        vmem((NZ, 8, HALF), F32),
        vmem((2, 8, HALF), F32),
        vmem((2, 2, HGA + HGB + HGC, BLOCK), BF16),
        vmem((ROWS, HALF), BF16),
    ]
    semaphores = [dma((5,)), dma((5,))]
    for n in (11, 1, 6, 16, 16, 12, 12, 32, 32, 32, 48, 46, 15, 3):
        semaphores += both(n)
    return buffers + semaphores


def local(tokens, codes, scales, norm_gain, key_grad):
    hbm, vmem = pl.BlockSpec(memory_space=pl.ANY), pl.BlockSpec(memory_space=pltpu.VMEM)
    keys, token_grad, weight_grad, gain_grad = pl.pallas_call(
        kernel,
        out_shape=(
            pltpu.VMEM((T, W), BF16),
            pltpu.VMEM((T, D), BF16),
            pltpu.VMEM((ROWS, W), F32),
            pltpu.VMEM((1, W), F32),
        ),
        in_specs=[hbm, vmem, vmem, vmem, hbm],
        out_specs=(vmem, vmem, vmem, vmem),
        scratch_shapes=scratch(),
        compiler_params=pltpu.CompilerParams(collective_id=0, has_side_effects=True, vmem_limit_bytes=58 << 20),
        cost_estimate=pl.CostEstimate(flops=6 * T * D * W, bytes_accessed=12 << 20, transcendentals=0),
    )(tokens, codes, scales.T, norm_gain.reshape(1, W), key_grad)
    return keys, token_grad, weight_grad, gain_grad.reshape(W)


def solution(mesh):
    return jax.shard_map(
        local,
        mesh=mesh,
        in_specs=(P(("dp", "fsdp"), None), P("fsdp", None), P("fsdp", None), P(), P(("dp", "fsdp"), None)),
        out_specs=(P(("dp", "fsdp"), None), P(("dp", "fsdp"), None), P("fsdp", None), P()),
        check_vma=False,
    )
```

time: 113 us -> 101 us (0.89)
  Pallas kernels: 103 us -> 96.5 us
  local copies, waits for them, and re-layouts: 9.11 us -> 4.12 us
    pallas_call x1, Pallas kernels: 103 us -> 96.5 us  [local(): pl.pallas_call(kernel, out_shape=(pltpu.VMEM((T, W), BF16), pltpu.VMEM((T...]
    unnamed x9 -> x4, local copies, waits for them, and re-layouts: 9.11 us -> 4.12 us
where the time goes in v2:
time: 101 us
  Pallas kernels  96.5 us (96%)
  local copies, waits for them, and re-layouts  4.12 us (4%)
    pallas_call x1, Pallas kernels, local(): pl.pallas_call(kernel, out_shape=(pltpu.VMEM((T, W), BF16), pltpu.VMEM((T...  96.5 us
    unnamed x4, local copies, waits for them, and re-layouts  4.12 us

profile of v2, /device:TPU:1, one launch (start us, length us, event | category | flops | bytes accessed | tf_op | source)
XLA Modules:
  0.0 101.3 jit_solution(9035821936745840007)
XLA Ops:
  0.6 96.5 %shard_map.84 = (bf16[384,1024]{1,0:T(8,128)(2,1)S(1)}, bf16[384,5120]{1,0:T(8,128)(2,1)S(1)}, f32[80,1024]{1,0:T(8,128)S(1)}, f32[1,1024]{1,0:T(1,128)S(1)}) custom-call(bf16[384,5120]{1,0:T(8,128)(2,1)} %tokens.1, bf16[80,1024]{1,0:T(8,128)(2,1)} %codes.1, f32[8,80]{1,0:T(8,128)} %bitcast.4, f32[1,1024]{1,0:T(1,128)} %bitcast.5, bf16[384,1024]{1,0:T(8,128)(2,1)} %key_grad.1), custom_call_target="tpu_custom_call" | custom-call | flops 12079595520 | bytes 12582912 | tf_op jit(solution)/shard_map/pallas_call | solution.py:830
  97.2 0.9 copy.13
  98.0 0.6 copy.16
  98.6 0.7 copy.15
  99.4 1.9 %copy.14 = bf16[384,5120]{1,0:T(8,128)(2,1)} copy(bf16[384,5120]{1,0:T(8,128)(2,1)S(1)} %get-tuple-element.13) | data formatting | bytes 7864320

commit v3 on v2

--- a/solution.py
+++ b/solution.py
@@ -14,7 +14,7 @@
 SLAB = 640
 PAIR = 2 * SLAB
 RA, RB, RC = 96, 96, 128
-GA, GB, GC = 96, 96, 128
+GA, GB, GC = 96, 128, 96
 NX, NY, NZ = 4, 4, 8
 UNITS = (1, 2, 3, 0)
 
@@ -133,8 +133,8 @@
 
     def m_az(d, s, u):
         sg = 1 - 2 * d
-        ref = wa.at[rem(z - sg * s, NZ), u]
-        at = (s * 2 + u) * 2 + d
+        ref = wa.at[rem(z - sg * s, NZ), u // 2, pl.ds(2 * (u % 2), 2)]
+        at = (s * 4 + u) * 2 + d
         return copy(ref, ref, s_az.at[at], r_az.at[at], dev(x, y, z + sg, core))
 
     def m_z(part, d, hops, begin):
@@ -253,8 +253,13 @@
     partner = x + 1 - 2 * xl
     fins = (dev(partner, y, z, core), sib, dev(partner, y, z, other))
 
-    def m_fin(i):
-        return copy(fin.at[xl, core], fin.at[xl, core], s_fin.at[i], r_fin.at[i], fins[i])
+    def m_fin(i, part):
+        ref = fin.at[xl, core, pl.ds((0, HGA, HGA + HGB)[part], (HGA, HGB, HGC)[part])]
+        return copy(ref, ref, s_fin.at[i * 3 + part], r_fin.at[i * 3 + part], fins[i])
+
+    def share(part):
+        for i in range(3):
+            m_fin(i, part).start()
 
     loop(4, lambda p: c_tok(p).start())
     c_kg().start()
@@ -379,24 +384,28 @@
         own_columns(part, (0, 1))
     for j in range(1, NY):
         m_ay(0, j).wait_recv()
-    for d in range(2):
-        m_az(d, 0, 0).start()
+    for u in (0, 1):
+        for d in range(2):
+            m_az(d, 0, u).start()
     far_z(1, True)
     own_columns(1, (2, 3))
     far_z(0, True)
     own_columns(0, (2, 3))
     for j in range(1, NY):
         m_ay(1, j).wait_recv()
-    for d in range(2):
-        m_az(d, 0, 1).start()
-    for d in range(2):
-        m_az(d, 0, 0).wait_recv()
-        m_az(d, 1, 0).start()
+    for u in (2, 3):
+        for d in range(2):
+            m_az(d, 0, u).start()
+    for u in (0, 1):
+        for d in range(2):
+            m_az(d, 0, u).wait_recv()
+            m_az(d, 1, u).start()
     loop(2, columns)
     loop(2, own_forward)
-    for d in range(2):
-        m_az(d, 0, 1).wait_recv()
-        m_az(d, 1, 1).start()
+    for u in (2, 3):
+        for d in range(2):
+            m_az(d, 0, u).wait_recv()
+            m_az(d, 1, u).start()
 
     def forward(k):
         for d in range(2):
@@ -413,14 +422,14 @@
     loop(4, later, 2)
 
     def ring(k):
-        for u in range(2):
+        for u in range(4):
             for d in range(2):
 
-                @pl.when(k < 2 + (u == d))
+                @pl.when(k < 2 + (u % 2 == d))
                 def _():
                     m_az(d, k + 1, u).wait_recv()
 
-                @pl.when(k < 1 + (u == d))
+                @pl.when(k < 1 + (u % 2 == d))
                 def _():
                     m_az(d, k + 2, u).start()
 
@@ -428,7 +437,9 @@
         def _():
             forward(k + 2)
 
-        transpose(k)
+        @pl.when(k < 4)
+        def _():
+            transpose(k)
 
         @pl.when(k > 0)
         def _():
@@ -441,9 +452,7 @@
                 m_cx(k, unit, d, 1).wait_recv()
                 m_by(k, unit, d, 1).wait_recv()
 
-    loop(4, ring)
-    last_hops(3)
-    consume(3)
+    loop(5, ring)
 
     gains = gain[0:1, pl.ds(pl.multiple_of(core * HALF, BLOCK), HALF)]
     lane = lax.broadcasted_iota(jnp.int32, (8, BLOCK), 1)
@@ -513,12 +522,8 @@
                     at = first // HGC
                     gc[2 * hh + at, zz, yy, first - at * HGC : last - at * HGC] = value
 
-        @pl.when(k < 2)
-        def _():
-            m_rc(k, e, 0).start()
-            m_rb(k, e, 0).start()
-            m_rc(k, 1 - e, 1).start()
-            m_rb(k, 1 - e, 1).start()
+        m_rc(k, e, 0).start()
+        m_rb(k, e, 0).start()
 
         @pl.when(t == 0)
         def _():
@@ -531,12 +536,6 @@
             def _():
                 for i in range(2):
                     m_a(d, d + 2 * i, 1, True).start()
-
-    loop(8, grad)
-    loop(2 * T // CH, norm_keys)
-    d_keys().start()
-    c_keys().start()
-    loop(NX, lambda j: m_gx(j).start(), 1)
 
     def finish(k):
         q = pair(3 - k)
@@ -612,13 +611,9 @@
             ref = rb.at[k, d, 0]
             ref[...] += gb[rem(y + sg, NY), 2 * q + d]
             m_rb(k, d, 2).start()
-
-        @pl.when(k < 2)
-        def _():
-            for what in range(2):
-                for d in range(2):
-                    m_rc(k + 2, d, what).start()
-                    m_rb(k + 2, d, what).start()
+        for d in range(2):
+            m_rc(k, d, 1).start()
+            m_rb(k, d, 1).start()
 
         for u in UNITS:
             for d in range(2):
@@ -630,8 +625,6 @@
                     raa[d, u, k] += ga[rem(z + sg * (3 - k), NZ), u]
                     m_a(d, u, k + 1).start()
 
-        token_part(k)
-
         @pl.when(k > 0)
         def _():
             finish(k - 1)
@@ -640,28 +633,44 @@
         def _():
             short(k - 2)
 
-        @pl.when(k == 0)
+        @pl.when(k == 1)
         def _():
             loop(NX, lambda j: m_gx(j).wait_recv(), 1)
             gy[y] = add(*(gx.at[i] for i in range(NX)))
             loop(NY, lambda j: m_gy(j).start(), 1)
 
-        @pl.when(k == 1)
+        @pl.when(k == 2)
         def _():
             loop(NY, lambda j: m_gy(j).wait_recv(), 1)
             gz[z] = add(*(gy.at[i] for i in range(NY)))
             for d in range(2):
                 m_gz(d, 0).start()
 
-        @pl.when(k > 1)
-        def _():
-            gain_step(k - 2)
-
-    loop(4, reduce)
-    m_gz(0, 2).wait_recv()
-    m_gz(1, 2).wait_recv()
-    m_gz(0, 3).start()
+        @pl.when(k == 3)
+        def _():
+            gain_step(0)
+
+        loop(k + k // 3, token_part, k - (k + 3) // 4)
+
+    def step(t):
+        @pl.when((t < 6) | (t == 7) | (t == 8))
+        def _():
+            grad(t - t // 7)
+
+        @pl.when(t == 9)
+        def _():
+            loop(2 * T // CH, norm_keys)
+            d_keys().start()
+            c_keys().start()
+            loop(NX, lambda j: m_gx(j).start(), 1)
+
+        @pl.when((t == 6) | (t > 8))
+        def _():
+            reduce((t - 6) - 2 * ((t - 6) // 3))
+
+    loop(12, step)
     finish(3)
+    gain_step(1)
     short(2)
     for u in UNITS:
         for d in range(2):
@@ -676,11 +685,15 @@
     ref[...] = add(ref, *(ray.at[i] for i in range(3))).astype(BF16)
     loop(NX, lambda j: m_rax(j).start(), 1)
     short(3)
-
-    m_gz(0, 3).wait_recv()
-    total = add(*(gz.at[i] for i in range(NZ)))
-    gfin[core] = jnp.broadcast_to(jnp.sum(total, axis=0, keepdims=True), (8, HALF))
-    m_gs().start()
+    m_gz(0, 2).wait_recv()
+    m_gz(1, 2).wait_recv()
+    m_gz(0, 3).start()
+
+    loop(NX, lambda j: m_rax(j).wait_recv(), 1)
+    mine = fin.at[xl, core]
+    own = ga.at[z, 0, xh, pl.ds(pl.multiple_of(xl * HGA, 16), HGA)]
+    mine[0:HGA] = add(own, *(rax.at[i] for i in range(3))).astype(BF16)
+    share(0)
 
     def token_sum(p):
         d_tg(p).wait()
@@ -690,19 +703,19 @@
         tg_out[:, cols] = (tokv[rows, cols].astype(F32) + tgr[:, cols].astype(F32)).astype(BF16)
 
     loop(4, token_sum)
-
-    loop(NX, lambda j: m_rax(j).wait_recv(), 1)
-    mine = fin.at[xl, core]
-    own = ga.at[z, 0, xh, pl.ds(pl.multiple_of(xl * HGA, 16), HGA)]
-    mine[0:HGA] = add(own, *(rax.at[i] for i in range(3))).astype(BF16)
     for d in range(2):
         m_rz(1, d, 3).wait_recv()
     mine[HGA + HGB :] = add(gc.at[x, z, y], rcz.at[0, 3], rcz.at[1, 3]).astype(BF16)
+    share(2)
     for d in range(2):
         m_rz(0, d, 3).wait_recv()
     mine[HGA : HGA + HGB] = add(gb.at[y, z, xh, xl], rbz.at[0, 3], rbz.at[1, 3]).astype(BF16)
-    for i in range(3):
-        m_fin(i).start()
+    share(1)
+    m_gz(0, 3).wait_recv()
+    total = add(*(gz.at[i] for i in range(NZ)))
+    gfin[core] = jnp.broadcast_to(jnp.sum(total, axis=0, keepdims=True), (8, HALF))
+    m_gs().start()
+
     m_ax().wait_send()
 
     def drain_y(j):
@@ -732,9 +745,9 @@
             for what in range(3):
                 m_rb(k, d, what).wait_send()
                 m_rc(k, d, what).wait_send()
-            for u in range(2):
-
-                @pl.when(k < 3 + (u == d))
+            for u in range(4):
+
+                @pl.when(k < 3 + (u % 2 == d))
                 def _():
                     m_az(d, k, u).wait_send()
 
@@ -771,7 +784,8 @@
     c_keys().wait()
 
     for i in range(3):
-        m_fin(i).wait()
+        for part in range(3):
+            m_fin(i, part).wait()
     m_gs().wait()
     for c in range(2):
         for half in range(2):
@@ -820,7 +834,7 @@
         vmem((ROWS, HALF), BF16),
     ]
     semaphores = [dma((5,)), dma((5,))]
-    for n in (11, 1, 6, 16, 16, 12, 12, 32, 32, 32, 48, 46, 15, 3):
+    for n in (11, 1, 6, 32, 16, 12, 12, 32, 32, 32, 48, 46, 15, 9):
         semaphores += both(n)
     return buffers + semaphores
 

time: 101 us -> 97.8 us (0.968)
  Pallas kernels: 96.5 us -> 92.9 us
    pallas_call x1, Pallas kernels: 96.5 us -> 92.9 us  [local(): pl.pallas_call(kernel, out_shape=(pltpu.VMEM((T, W), BF16), pltpu.VMEM((T...]
where the time goes in v3:
time: 97.8 us; the launch traced here: 97.7 us
  Pallas kernels  92.9 us (95%)
  local copies, waits for them, and re-layouts  4.12 us (4%)
    pallas_call x1, Pallas kernels, local(): pl.pallas_call(kernel, out_shape=(pltpu.VMEM((T, W), BF16), pltpu.VMEM((T...  92.9 us
    unnamed x4, local copies, waits for them, and re-layouts  4.12 us

profile of v3, /device:TPU:1, one launch (start us, length us, event | category | flops | bytes accessed | tf_op | source)
XLA Modules:
  0.0 97.7 jit_solution(14095524221205864604)
XLA Ops:
  0.6 92.9 %shard_map.84 = (bf16[384,1024]{1,0:T(8,128)(2,1)S(1)}, bf16[384,5120]{1,0:T(8,128)(2,1)S(1)}, f32[80,1024]{1,0:T(8,128)S(1)}, f32[1,1024]{1,0:T(1,128)S(1)}) custom-call(bf16[384,5120]{1,0:T(8,128)(2,1)} %tokens.1, bf16[80,1024]{1,0:T(8,128)(2,1)} %codes.1, f32[8,80]{1,0:T(8,128)} %bitcast.4, f32[1,1024]{1,0:T(1,128)} %bitcast.5, bf16[384,1024]{1,0:T(8,128)(2,1)} %key_grad.1), custom_call_target="tpu_custom_call" | custom-call | flops 12079595520 | bytes 12582912 | tf_op jit(solution)/shard_map/pallas_call | solution.py:844
  93.6 0.9 copy.13
  94.5 0.6 copy.16
  95.0 0.7 copy.15
  95.8 1.9 %copy.14 = bf16[384,5120]{1,0:T(8,128)(2,1)} copy(bf16[384,5120]{1,0:T(8,128)(2,1)S(1)} %get-tuple-element.13) | data formatting | bytes 7864320

commit v4 on v3

--- a/solution.py
+++ b/solution.py
@@ -13,7 +13,7 @@
 HALF = W // 2
 SLAB = 640
 PAIR = 2 * SLAB
-RA, RB, RC = 96, 96, 128
+RA, RB, RC = 96, 128, 96
 GA, GB, GC = 96, 128, 96
 NX, NY, NZ = 4, 4, 8
 UNITS = (1, 2, 3, 0)
@@ -261,9 +261,6 @@
         for i in range(3):
             m_fin(i, part).start()
 
-    loop(4, lambda p: c_tok(p).start())
-    c_kg().start()
-
     barrier = pltpu.get_barrier_semaphore()
 
     def signal(device):
@@ -295,6 +292,8 @@
                 if first // HC == mine:
                     wc[x, z, 0, first - mine * HC : last - mine * HC] = stage[row : row + last - first, column(block)]
 
+    loop(4, lambda p: c_tok(p).start())
+    c_kg().start()
     pl.semaphore_wait(barrier, 12)
     m_ax().start()
     for j in range(1, NY):
@@ -415,9 +414,11 @@
             m_by(k, 1, d, 1).start()
 
     def later(k):
+        transpose(2 * k - 4)
         columns(k)
         forward(k - 2)
         own_forward(k)
+        transpose(2 * k - 3)
 
     loop(4, later, 2)
 
@@ -436,10 +437,6 @@
         @pl.when(k < 2)
         def _():
             forward(k + 2)
-
-        @pl.when(k < 4)
-        def _():
-            transpose(k)
 
         @pl.when(k > 0)
         def _():

time: 97.8 us -> 96.9 us (level)
  no operation moved by 1% of the time
where the time goes in v4:
time: 96.9 us; the launch traced here: 96.8 us
  Pallas kernels  92 us (95%)
  local copies, waits for them, and re-layouts  4.12 us (4%)
    pallas_call x1, Pallas kernels, local(): pl.pallas_call(kernel, out_shape=(pltpu.VMEM((T, W), BF16), pltpu.VMEM((T...  92 us
    unnamed x4, local copies, waits for them, and re-layouts  4.12 us

profile of v4, /device:TPU:1, one launch (start us, length us, event | category | flops | bytes accessed | tf_op | source)
XLA Modules:
  0.0 96.8 jit_solution(17275055454510831836)
XLA Ops:
  0.6 92.0 %shard_map.84 = (bf16[384,1024]{1,0:T(8,128)(2,1)S(1)}, bf16[384,5120]{1,0:T(8,128)(2,1)S(1)}, f32[80,1024]{1,0:T(8,128)S(1)}, f32[1,1024]{1,0:T(1,128)S(1)}) custom-call(bf16[384,5120]{1,0:T(8,128)(2,1)} %tokens.1, bf16[80,1024]{1,0:T(8,128)(2,1)} %codes.1, f32[8,80]{1,0:T(8,128)} %bitcast.4, f32[1,1024]{1,0:T(1,128)} %bitcast.5, bf16[384,1024]{1,0:T(8,128)(2,1)} %key_grad.1), custom_call_target="tpu_custom_call" | custom-call | flops 12079595520 | bytes 12582912 | tf_op jit(solution)/shard_map/pallas_call | solution.py:841
  92.7 0.9 copy.13
  93.6 0.6 copy.16
  94.1 0.7 copy.15
  94.9 1.9 %copy.14 = bf16[384,5120]{1,0:T(8,128)(2,1)} copy(bf16[384,5120]{1,0:T(8,128)(2,1)S(1)} %get-tuple-element.13) | data formatting | bytes 7864320
